TPU v7x, 32 devices: a whole 2x2x4 slice. The times are simulated.
32 devices in a mesh: dp: 4 (over z), blk: 2 (over y), ulysses: 4 (over x, core).
Axes of the slice: x: 2, y: 2, z: 4, core: 2. Of those that a mesh axis runs over, the one named last changes fastest.
Arguments:
- inputs: bfloat16 [4, 1024, 1024], P('dp', ('blk', 'ulysses')), may hold values from -6 to 6
- gain_attn: float32 [1024], replicated, may hold values from 0.1 to 1.9
- query_key_value_weight: bfloat16 [1024, 2048], P(('dp', 'blk')), may hold values from -0.1875 to 0.1875
- w_out: bfloat16 [1024, 1024], P(('dp', 'blk')), may hold values from -4 to 4
- gain_mix: float32 [1024], replicated, may hold values from 0.1 to 1.9
- router: bfloat16 [1024, 16], replicated, may hold values from -0.09375 to 0.09375
- expert_in: bfloat16 [16, 1024, 1024], P(('dp', 'blk')), may hold values from -0.1875 to 0.1875
- expert_down: bfloat16 [16, 512, 1024], P(('dp', 'blk')), may hold values from -2 to 2
- routes: int32 [4, 1024, 8], P('dp', ('blk', 'ulysses')), may hold values from 0 to 15, all different within a row; in each aligned block of 128 rows (0 to 127, 128 to 255, ..., all dimensions but the last counted through in order) at most 80 rows name the same one
- cotangent: bfloat16 [4, 1024, 1024], P('dp', ('blk', 'ulysses')), may hold values from -6 to 6
Outputs:
- result: bfloat16 [4, 1024, 1024], P('dp', ('blk', 'ulysses'))
- input_grad: bfloat16 [4, 1024, 1024], P('dp', ('blk', 'ulysses'))
- grad_gain_attn: float32 [1024], replicated
- grad_w_qkv: float32 [1024, 2048], P(('dp', 'blk'))
- grad_w_out: float32 [1024, 1024], P(('dp', 'blk'))
- grad_gain_mix: float32 [1024], replicated
- grad_router: float32 [1024, 16], replicated
- grad_expert_in: float32 [16, 1024, 1024], P(('dp', 'blk'))
- grad_expert_down: float32 [16, 512, 1024], P(('dp', 'blk'))
Inputs may be any that keep to these rules, and one draw needn't show every extreme that they name: `routes`: each row names 8 different experts. Within the 128 rows of one device no expert is named by more than 80 rows, and in some devices' rows one expert is named by exactly 80.
All inputs are finite; a program needn't handle non-finite values.
Results may differ from a plain program's by a relative error of at most 0.019.
Values may be sent and summed in bfloat16 or wider, within the bound.
A program may use at most 192 MiB of HBM per device.

v0:
```python
import math

import jax
import jax.numpy as jnp
from jax import lax
from jax.sharding import PartitionSpec as P

QUERY_HEADS = 16
KEY_VALUE_HEADS = 8
HEAD_SIZE = 64
CAPACITY = 80


EPSILON = 1e-06
THETA = 10000.0
MASKED = -1e30


def passed_along(value, axis, steps):
    count = lax.axis_size(axis)
    initial, last = (max(0, -steps), min(count, count - steps))
    return lax.ppermute(value, axis, [(source, source + steps) for source in range(initial, last)])


def rms_scale(values, gain):
    return values * lax.rsqrt(jnp.mean(values * values, axis=-1, keepdims=True) + EPSILON) * gain


def rotary_tables(positions, head_width):
    exponent = jnp.arange(head_width // 2, dtype=jnp.float32) * (2.0 / head_width)
    inverse = jnp.exp(-math.log(THETA) * exponent)
    angles = positions.astype(jnp.float32)[:, None] * inverse[None, :]
    return (jnp.cos(angles)[:, None, :], jnp.sin(angles)[:, None, :])


def rotate(values, cosine, sine):
    half_size = values.shape[-1] // 2
    first_half = values[..., :half_size]
    second_half = values[..., half_size:]
    return jnp.concatenate(
        [first_half * cosine - second_half * sine, second_half * cosine + first_half * sine],
        axis=-1,
    )


def rotate_back(grad_values, cosine, sine):
    half_size = grad_values.shape[-1] // 2
    first_half = grad_values[..., :half_size]
    second_half = grad_values[..., half_size:]
    return jnp.concatenate(
        [first_half * cosine + second_half * sine, second_half * cosine - first_half * sine],
        axis=-1,
    )


def attend_forward(queries, all_keys, all_values, query_pos, key_pos, key_ok, row_block):
    score_scale = queries.shape[-1] ** (-0.5)
    block_count = queries.shape[0] // row_block

    def one_block(block_index):
        offset = block_index * row_block
        row_part = lax.dynamic_slice_in_dim(queries, offset, row_block, 0)
        query_here = lax.dynamic_slice_in_dim(query_pos, offset, row_block, 0)
        scores = (
            jnp.einsum("qrgd,krd->qrgk", row_part, all_keys, preferred_element_type=jnp.float32)
            * score_scale
        )
        allowed = (key_pos[None, :] <= query_here[:, None]) & key_ok[None, :]
        scores = jnp.where(allowed[:, None, None, :], scores, MASKED)
        row_peak = jnp.max(scores, axis=-1, keepdims=True)
        exps_all = jnp.exp(scores - row_peak)
        row_total = jnp.sum(exps_all, axis=-1, keepdims=True)
        weights_low = (exps_all / row_total).astype(jnp.bfloat16)
        mixed_part = jnp.einsum(
            "qrgk,krd->qrgd", weights_low, all_values, preferred_element_type=jnp.float32
        )
        return (mixed_part, (row_peak + jnp.log(row_total))[..., 0])

    mixed_blocks, log_sums = lax.map(one_block, jnp.arange(block_count, dtype=jnp.int32))
    return (mixed_blocks.reshape(queries.shape), log_sums.reshape(queries.shape[:3]))


def attend_backward(
    queries, all_keys, all_values, query_pos, key_pos, key_ok, log_sums, mixed_grad, row_block
):
    score_scale = queries.shape[-1] ** (-0.5)
    block_count = queries.shape[0] // row_block

    def one_block(carry, block_index):
        key_grads, value_grads = carry
        offset = block_index * row_block
        row_part = lax.dynamic_slice_in_dim(queries, offset, row_block, 0)
        query_here = lax.dynamic_slice_in_dim(query_pos, offset, row_block, 0)
        grad_part = lax.dynamic_slice_in_dim(mixed_grad, offset, row_block, 0)
        sums_part = lax.dynamic_slice_in_dim(log_sums, offset, row_block, 0)
        scores = (
            jnp.einsum("qrgd,krd->qrgk", row_part, all_keys, preferred_element_type=jnp.float32)
            * score_scale
        )
        allowed = (key_pos[None, :] <= query_here[:, None]) & key_ok[None, :]
        scores = jnp.where(allowed[:, None, None, :], scores, MASKED)
        probs_all = jnp.exp(scores - sums_part[..., None])
        value_grads = value_grads + jnp.einsum(
            "qrgk,qrgd->krd",
            probs_all.astype(jnp.bfloat16),
            grad_part,
            preferred_element_type=jnp.float32,
        )
        probs_grad = jnp.einsum(
            "qrgd,krd->qrgk", grad_part, all_values, preferred_element_type=jnp.float32
        )
        score_grad = probs_all * (
            probs_grad - jnp.sum(probs_all * probs_grad, axis=-1, keepdims=True)
        )
        score_low = score_grad.astype(jnp.bfloat16)
        row_grads = (
            jnp.einsum("qrgk,krd->qrgd", score_low, all_keys, preferred_element_type=jnp.float32)
            * score_scale
        )
        key_grads = (
            key_grads
            + jnp.einsum("qrgk,qrgd->krd", score_low, row_part, preferred_element_type=jnp.float32)
            * score_scale
        )
        return ((key_grads, value_grads), row_grads)

    zero_grads = jnp.zeros(all_keys.shape, jnp.float32)
    (key_grads, value_grads), row_grads = lax.scan(
        one_block, (zero_grads, zero_grads), jnp.arange(block_count, dtype=jnp.int32)
    )
    return (row_grads.reshape(queries.shape), key_grads, value_grads)


def expert_backward(row_part, weight_in, weight_down, out_grads):
    hidden_units = weight_down.shape[1]
    both_halves = jnp.einsum(
        "ecd,edf->ecf", row_part, weight_in, preferred_element_type=jnp.float32
    )
    gate_half = both_halves[..., :hidden_units]
    up_half = both_halves[..., hidden_units:]
    sigmoid_gate = jax.nn.sigmoid(gate_half)
    activated = gate_half * sigmoid_gate
    hidden = (activated * up_half).astype(jnp.bfloat16)
    hidden_grad = jnp.einsum(
        "ecd,ehd->ech", out_grads, weight_down, preferred_element_type=jnp.float32
    )
    gate_grad = hidden_grad * up_half * sigmoid_gate * (1.0 + gate_half * (1.0 - sigmoid_gate))
    up_grad = hidden_grad * activated
    both_grad = jnp.concatenate([gate_grad, up_grad], axis=-1).astype(jnp.bfloat16)
    row_grads = jnp.einsum("ecf,edf->ecd", both_grad, weight_in, preferred_element_type=jnp.float32)
    return (row_grads, both_grad, hidden)


def expert_whole(row_part, weight_in, weight_down, out_grads):
    row_grads, both_grad, hidden = expert_backward(row_part, weight_in, weight_down, out_grads)
    expert_out = jnp.einsum("ech,ehd->ecd", hidden, weight_down, preferred_element_type=jnp.float32)
    return (expert_out, row_grads, both_grad, hidden)


def expert_terms(row_data, hidden, both_grad, expert_grad, width, hidden_units, total_rows):
    count = row_data.shape[0]
    per_expert = width + hidden_units
    left_rows = jnp.concatenate(
        [jnp.transpose(row_data, (0, 2, 1)), jnp.transpose(hidden, (0, 2, 1))], axis=1
    ).reshape(count * per_expert, row_data.shape[1])
    right_sides = jnp.stack([both_grad, expert_grad], axis=1)
    row_group = math.gcd(math.gcd(width, hidden_units), total_rows)

    def expert_term(offset, row_count):

        def one_group(group_index):
            first_row = group_index * row_group
            left_part = lax.dynamic_slice_in_dim(left_rows, first_row, row_group, 0)
            expert_id = first_row // per_expert
            half_index = (first_row % per_expert >= width).astype(jnp.int32)
            right_part = right_sides[expert_id, half_index]
            return jnp.dot(left_part, right_part, preferred_element_type=jnp.float32)

        group_terms = lax.map(one_group, jnp.arange(row_count // row_group, dtype=jnp.int32))
        return group_terms.reshape(row_count, right_sides.shape[-1])

    return expert_term


def body(
    inputs,
    gain_attn,
    query_key_value_weight,
    w_out,
    gain_mix,
    router,
    expert_in,
    expert_down,
    routes,
    cotangent,
):
    cycle_size = lax.axis_size("blk")
    slice_total = lax.axis_size("ulysses")
    devices = lax.axis_size("dp") * cycle_size * slice_total
    cycle_index = lax.axis_index("blk")
    slice_index = lax.axis_index("ulysses")
    token_rows = inputs.shape[1]
    width = inputs.shape[2]
    head_width = HEAD_SIZE
    head_copies = max(1, slice_total // KEY_VALUE_HEADS)
    repeated_heads = KEY_VALUE_HEADS * head_copies
    group_size = QUERY_HEADS // repeated_heads
    local_rep = repeated_heads // slice_total
    local_query = QUERY_HEADS // slice_total
    span_len = token_rows * slice_total
    row_block = min(512, span_len)
    query_columns = QUERY_HEADS * head_width
    key_value_columns = KEY_VALUE_HEADS * head_width
    num_experts = router.shape[1]
    top_count = routes.shape[2]
    capacity = CAPACITY
    hidden_units = expert_down.shape[1]
    layer_in = inputs[0].astype(jnp.float32)
    norm_attn = rms_scale(layer_in, gain_attn).astype(jnp.bfloat16)
    qkv_full, out_full = (
        lax.all_gather(query_key_value_weight, ("dp", "blk"), axis=0, tiled=True),
        lax.all_gather(w_out, ("dp", "blk"), axis=0, tiled=True),
    )
    projected_rows = jnp.dot(norm_attn, qkv_full, preferred_element_type=jnp.float32)
    positions = (cycle_index * slice_total + slice_index) * token_rows + jnp.arange(
        token_rows, dtype=jnp.int32
    )
    cosine, sine = rotary_tables(positions, head_width)
    q_raw = projected_rows[:, :query_columns].reshape(token_rows, QUERY_HEADS, head_width)
    key_plain = projected_rows[:, query_columns : query_columns + key_value_columns].reshape(
        token_rows, KEY_VALUE_HEADS, head_width
    )
    value_plain = projected_rows[:, query_columns + key_value_columns :].reshape(
        token_rows, KEY_VALUE_HEADS, head_width
    )
    q_send = (
        rotate(q_raw, cosine, sine)
        .astype(jnp.bfloat16)
        .reshape(token_rows, slice_total, local_query * head_width)
    )
    k_send = (
        jnp.repeat(rotate(key_plain, cosine, sine), head_copies, axis=1)
        .astype(jnp.bfloat16)
        .reshape(token_rows, slice_total, local_rep * head_width)
    )
    v_send = (
        jnp.repeat(value_plain, head_copies, axis=1)
        .astype(jnp.bfloat16)
        .reshape(token_rows, slice_total, local_rep * head_width)
    )
    q_heads, k_heads, v_heads = (
        lax.all_to_all(q_send, "ulysses", split_axis=1, concat_axis=0, tiled=True),
        lax.all_to_all(k_send, "ulysses", split_axis=1, concat_axis=0, tiled=True),
        lax.all_to_all(v_send, "ulysses", split_axis=1, concat_axis=0, tiled=True),
    )
    queries = q_heads.reshape(span_len, local_rep, group_size, head_width)
    own_pair = jnp.stack(
        [
            k_heads.reshape(span_len, local_rep, head_width),
            v_heads.reshape(span_len, local_rep, head_width),
        ]
    )
    pair_list = [own_pair]
    cycle_step = 1
    pair_list.append(passed_along(own_pair, "blk", cycle_step))
    all_keys = jnp.concatenate([pair_item[0] for pair_item in pair_list], axis=0)
    all_values = jnp.concatenate([pair_item[1] for pair_item in pair_list], axis=0)
    span_rows = jnp.arange(span_len, dtype=jnp.int32)
    key_pos = jnp.concatenate(
        [(cycle_index - cycle_step) * span_len + span_rows for cycle_step in range(cycle_size)]
    )
    key_ok = jnp.concatenate(
        [
            jnp.broadcast_to(cycle_index - cycle_step >= 0, (span_len,))
            for cycle_step in range(cycle_size)
        ]
    )
    query_pos = cycle_index * span_len + span_rows
    attn_heads, log_sums = attend_forward(
        queries, all_keys, all_values, query_pos, key_pos, key_ok, row_block
    )
    mixed_send = attn_heads.astype(jnp.bfloat16).reshape(span_len, 1, local_query * head_width)
    attn_mixed = lax.all_to_all(
        mixed_send, "ulysses", split_axis=0, concat_axis=1, tiled=True
    ).reshape(token_rows, query_columns)
    branch = lax.dot_general(
        attn_mixed, out_full, (((1,), (1,)), ((), ())), preferred_element_type=jnp.float32
    )
    residual = layer_in + branch
    norm_mix = rms_scale(residual, gain_mix).astype(jnp.bfloat16)
    logits = jnp.dot(norm_mix, router, preferred_element_type=jnp.float32)
    route_ids = routes[0]
    route_picks = (
        route_ids[:, :, None] == jnp.arange(num_experts, dtype=jnp.int32)[None, None, :]
    ).astype(jnp.float32)
    chosen = jnp.sum(route_picks * logits[:, None, :], axis=-1)
    gate_values = jax.nn.softmax(chosen, axis=-1)
    flat_routes = route_ids.reshape(-1)
    marks = (flat_routes[:, None] == jnp.arange(num_experts, dtype=jnp.int32)[None, :]).astype(
        jnp.int32
    )
    filled = jnp.cumsum(marks, axis=0)
    slot_number = jnp.sum(marks * filled, axis=1) - 1
    slot_index = flat_routes * capacity + slot_number
    token_ids = jnp.arange(token_rows * top_count, dtype=jnp.int32) // top_count
    slot_owner = (
        jnp.full((num_experts * capacity,), token_rows, jnp.int32).at[slot_index].set(token_ids)
    )
    padded = jnp.concatenate([norm_mix, jnp.zeros((1, width), jnp.bfloat16)], axis=0)
    dispatched = padded[slot_owner].reshape(num_experts, capacity, width)
    out_grad = cotangent[0].astype(jnp.float32)
    route_grads = (gate_values[..., None] * out_grad[:, None, :]).reshape(
        token_rows * top_count, width
    )
    expert_grad = (
        jnp.zeros((num_experts * capacity, width), jnp.float32).at[slot_index].set(route_grads)
    )
    expert_grad = expert_grad.astype(jnp.bfloat16).reshape(num_experts, capacity, width)
    held_rows, held_grads = (
        lax.all_to_all(dispatched, ("dp", "blk"), split_axis=0, concat_axis=1, tiled=True),
        lax.all_to_all(expert_grad, ("dp", "blk"), split_axis=0, concat_axis=1, tiled=True),
    )
    held_out, held_row_grads, held_both, held_hidden = expert_whole(
        held_rows, expert_in, expert_down, held_grads
    )
    expert_out, dispatch_grad = (
        lax.all_to_all(
            held_out.astype(jnp.bfloat16), ("dp", "blk"), split_axis=1, concat_axis=0, tiled=True
        ).astype(held_out.dtype),
        lax.all_to_all(
            held_row_grads.astype(jnp.bfloat16),
            ("dp", "blk"),
            split_axis=1,
            concat_axis=0,
            tiled=True,
        ).astype(held_row_grads.dtype),
    )
    routed = expert_out.reshape(num_experts * capacity, width)[slot_index].reshape(
        token_rows, top_count, width
    )
    result = (residual + jnp.sum(gate_values[..., None] * routed, axis=1)).astype(jnp.bfloat16)
    gate_grad = jnp.sum(out_grad[:, None, :] * routed, axis=-1)
    chosen_grad = gate_values * (
        gate_grad - jnp.sum(gate_values * gate_grad, axis=-1, keepdims=True)
    )
    logit_grad = jnp.sum(chosen_grad[..., None] * route_picks, axis=1)
    mix_grad = jnp.sum(
        dispatch_grad.reshape(num_experts * capacity, width)[slot_index].reshape(
            token_rows, top_count, width
        ),
        axis=1,
    )
    router_wide = router.astype(jnp.float32)
    mix_grad = mix_grad + jnp.dot(logit_grad, router_wide.T, precision=lax.Precision.HIGHEST)
    router_grad = jnp.dot(
        norm_mix.astype(jnp.float32).T, logit_grad, precision=lax.Precision.HIGHEST
    )
    _, mix_back = jax.vjp(rms_scale, residual, gain_mix)
    residual_norm_grad, gain_mix_grad = mix_back(mix_grad)
    residual_grad = out_grad + residual_norm_grad
    branch_grad = residual_grad.astype(jnp.bfloat16)
    mixed_tok_grad = jnp.dot(branch_grad, out_full, preferred_element_type=jnp.float32)
    mixed_send_grad = mixed_tok_grad.astype(jnp.bfloat16).reshape(
        token_rows, slice_total, local_query * head_width
    )
    mixed_grad = lax.all_to_all(
        mixed_send_grad, "ulysses", split_axis=1, concat_axis=0, tiled=True
    ).reshape(span_len, local_rep, group_size, head_width)
    query_grad, key_grads, value_grads = attend_backward(
        queries, all_keys, all_values, query_pos, key_pos, key_ok, log_sums, mixed_grad, row_block
    )
    pair_grads = jnp.stack([key_grads, value_grads]).reshape(
        2, cycle_size, span_len, local_rep, head_width
    )
    own_grads = pair_grads[:, 0]
    cycle_step = 1
    own_grads = own_grads + passed_along(
        pair_grads[:, cycle_step].astype(jnp.bfloat16), "blk", -cycle_step
    ).astype(jnp.float32)
    dq_send = query_grad.astype(jnp.bfloat16).reshape(span_len, 1, local_query * head_width)
    dk_send = own_grads[0].astype(jnp.bfloat16).reshape(span_len, 1, local_rep * head_width)
    dv_send = own_grads[1].astype(jnp.bfloat16).reshape(span_len, 1, local_rep * head_width)
    dq_tok, key_gradient_tokens, value_gradient_tokens = (
        lax.all_to_all(dq_send, "ulysses", split_axis=0, concat_axis=1, tiled=True),
        lax.all_to_all(dk_send, "ulysses", split_axis=0, concat_axis=1, tiled=True),
        lax.all_to_all(dv_send, "ulysses", split_axis=0, concat_axis=1, tiled=True),
    )
    dq_raw = rotate_back(
        dq_tok.astype(jnp.float32).reshape(token_rows, QUERY_HEADS, head_width), cosine, sine
    )
    key_gradient_sum = jnp.sum(
        key_gradient_tokens.astype(jnp.float32).reshape(
            token_rows, KEY_VALUE_HEADS, head_copies, head_width
        ),
        axis=2,
    )
    dk_raw = rotate_back(key_gradient_sum, cosine, sine)
    value_gradient_plain = jnp.sum(
        value_gradient_tokens.astype(jnp.float32).reshape(
            token_rows, KEY_VALUE_HEADS, head_copies, head_width
        ),
        axis=2,
    )
    qkv_grad = jnp.concatenate(
        [
            dq_raw.reshape(token_rows, query_columns),
            dk_raw.reshape(token_rows, key_value_columns),
            value_gradient_plain.reshape(token_rows, key_value_columns),
        ],
        axis=1,
    ).astype(jnp.bfloat16)
    attn_norm_grad = lax.dot_general(
        qkv_grad, qkv_full, (((1,), (1,)), ((), ())), preferred_element_type=jnp.float32
    )
    _, attn_back = jax.vjp(rms_scale, layer_in, gain_attn)
    input_norm_grad, gain_attn_grad = attn_back(attn_norm_grad)
    input_grad = (residual_grad + input_norm_grad).astype(jnp.bfloat16)
    qkv_term = lax.dot_general(
        norm_attn, qkv_grad, (((0,), (0,)), ((), ())), preferred_element_type=jnp.float32
    )
    out_term = lax.dot_general(
        branch_grad, attn_mixed, (((0,), (0,)), ((), ())), preferred_element_type=jnp.float32
    )
    attn_part = lax.psum_scatter(
        jnp.concatenate([qkv_term, out_term], axis=1),
        ("dp", "blk", "ulysses"),
        scatter_dimension=0,
        tiled=True,
    )
    per_expert = width + hidden_units
    expert_rows = num_experts * per_expert // devices
    held_term = expert_terms(
        held_rows, held_hidden, held_both, held_grads, width, hidden_units, expert_rows
    )
    expert_part = lax.psum_scatter(
        held_term(jnp.int32(0), expert_rows * lax.axis_size("ulysses")).astype(jnp.bfloat16),
        "ulysses",
        scatter_dimension=0,
        tiled=True,
    ).astype(jnp.float32)
    attn_shard, expert_shard = (
        lax.all_gather(attn_part.astype(jnp.bfloat16), "ulysses", axis=0, tiled=True).astype(
            attn_part.dtype
        ),
        lax.all_gather(expert_part.astype(jnp.bfloat16), "ulysses", axis=0, tiled=True).astype(
            expert_part.dtype
        ),
    )
    gain_attn_grad, gain_mix_grad, router_grad = lax.psum(
        (gain_attn_grad, gain_mix_grad, router_grad), ("dp", "blk", "ulysses")
    )
    qkv_width = query_key_value_weight.shape[1]
    grad_w_qkv = attn_shard[:, :qkv_width]
    grad_w_out = attn_shard[:, qkv_width:]
    expert_blocks = expert_shard.reshape(expert_in.shape[0], per_expert, expert_in.shape[2])
    grad_expert_in = expert_blocks[:, :width]
    grad_expert_down = expert_blocks[:, width:]
    return (
        result[None],
        input_grad[None],
        gain_attn_grad,
        grad_w_qkv,
        grad_w_out,
        gain_mix_grad,
        router_grad,
        grad_expert_in,
        grad_expert_down,
    )


def solution(mesh):
    in_specs = (
        P("dp", ("blk", "ulysses"), None),
        P(),
        P(("dp", "blk"), None),
        P(("dp", "blk"), None),
        P(),
        P(),
        P(("dp", "blk"), None, None),
        P(("dp", "blk"), None, None),
        P("dp", ("blk", "ulysses"), None),
        P("dp", ("blk", "ulysses"), None),
    )
    out_specs = (
        P("dp", ("blk", "ulysses"), None),
        P("dp", ("blk", "ulysses"), None),
        P(),
        P(("dp", "blk"), None),
        P(("dp", "blk"), None),
        P(),
        P(),
        P(("dp", "blk"), None, None),
        P(("dp", "blk"), None, None),
    )
    return jax.shard_map(body, mesh=mesh, in_specs=in_specs, out_specs=out_specs, check_vma=False)
```

profile of v0, /device:TPU:1, one launch (start us, length us, event | category | flops | bytes accessed | tf_op | source)
XLA Modules:
  0.0 870.5 jit_solution(922253844831511777)
XLA Ops:
  12.2 4.5 reduce-window.6
  17.5 4.9 scatter_custom_fusion
  22.3 62.1 %all-gather.4.cloned.1.call-done = bf16[1024,2048]{1,0:T(8,128)(2,1)} async-done(((bf16[128,2048]{1,0:T(8,128)(2,1)}), bf16[1024,2048]{1,0:T(8,128)(2,1)}) %all-gather.4.cloned.1.call-update) | async-done | bytes 4194320 | tf_op jit(solution)/shard_map/all_gather | solution.py:221
  84.5 3.1 fusion.57
  88.5 5.2 all-to-all-start
  94.5 3.2 all-to-all-done
  97.7 3.9 all-to-all-start.1
  101.9 3.3 all-to-all-done.1
  109.4 4.3 all-to-all-start.2
  115.3 3.6 all-to-all-done.2
  119.4 2.8 fusion.79
  129.4 4.1 all-to-all-start.3
  134.2 4.6 all-to-all-done.3
  143.9 5.1 gather_fusion
  149.0 5.0 all-to-all-start.4
  157.3 8.1 scatter_custom_fusion.1
  165.4 4.5 convert_element_type.265
  169.8 42.9 %all-to-all-done.4 = bf16[16,80,1024]{2,1,0:T(8,128)(2,1)} async-done(((bf16[16,80,1024]{2,1,0:T(8,128)(2,1)}), bf16[16,80,1024]{2,1,0:T(8,128)(2,1)}, u32[]{:S(2)}, u32[]{:S(2)}) %all-to-all-start.4) | async-done | bytes 2621472 | tf_op jit(solution)/shard_map/all_to_all | solution.py:320
  212.7 4.6 all-to-all-start.6
  217.3 3.6 copy.220
  220.9 54.7 %all-to-all-done.6 = bf16[16,80,1024]{2,1,0:T(8,128)(2,1)} async-done(((bf16[16,80,1024]{2,1,0:T(8,128)(2,1)}), bf16[16,80,1024]{2,1,0:T(8,128)(2,1)}, u32[]{:S(2)}, u32[]{:S(2)}) %all-to-all-start.6) | async-done | bytes 2621472 | tf_op jit(solution)/shard_map/all_to_all | solution.py:321
  278.0 5.2 fusion.81
  283.3 3.7 multiply_convert_fusion.1
  287.0 3.1 fusion.25
  290.1 4.2 copy.227
  294.4 5.4 all-to-all-start.7
  299.8 2.8 convolution_convert_fusion
  302.7 4.2 copy.221
  309.1 6.5 copy.247
  315.6 5.2 pad_maximum_fusion.1
  320.8 37.1 %all-to-all-done.7 = bf16[2,640,1024]{2,0,1:T(2,128)(2,1)} async-done(((bf16[2,640,1024]{2,0,1:T(2,128)(2,1)}), bf16[2,640,1024]{2,0,1:T(2,128)(2,1)}, u32[]{:S(2)}, u32[]{:S(2)}) %all-to-all-start.7) | async-done | bytes 2621472 | tf_op jit(solution)/shard_map/all_to_all | solution.py:330
  357.9 5.2 all-to-all-start.5
  363.2 49.1 %while.8 = (s32[]{:T(128)}, bf16[12,256,1024]{2,1,0:T(8,128)(2,1)}, s32[12]{0:T(128)S(1)}, bf16[3072,640]{1,0:T(8,128)(2,1)}, bf16[2,2,640,1024]{3,2,0,1:T(8,128...) while((s32[]{:T(128)}, ...), condition=%wide.region_27.28_spmd, body=%wide.region_26.27_spmd.sunk | while | flops 335544352 | bytes 2687380 | solution.py:179
  364.5 2.8 fusion.114
  376.7 2.8 fusion.114
  380.8 2.8 fusion.114
  389.0 2.8 fusion.114
  401.2 2.8 fusion.114
  405.3 2.8 fusion.114
  412.3 5.0 copy.228
  417.3 4.0 all-to-all-done.5
  421.3 5.7 copy.222
  427.0 9.0 %gather_fusion.2 = f32[1024,1024]{1,0:T(8,128)} fusion(f32[1280,1024]{1,0:T(8,128)} %bitcast.241, s32[1024]{0:T(1024)S(1)} %broadcast_clamp_fusion), kind=kCustom, calls=%fused_computation.2 | custom fusion | bytes 8392704 | tf_op jit(solution)/shard_map/gather | solution.py:348
  435.9 9.0 %gather_fusion.1 = f32[1024,1024]{1,0:T(8,128)} fusion(f32[1280,1024]{1,0:T(8,128)} %bitcast.242, s32[1024]{0:T(1024)S(1)} %broadcast_clamp_fusion), kind=kCustom, calls=%fused_computation.1 | custom fusion | bytes 8392704 | tf_op jit(solution)/shard_map/gather | solution.py:338
  445.0 4.7 fusion.14
  449.8 3.4 bitcast_reduce_fusion
  457.0 5.6 all-to-all-start.8
  463.3 7.6 all-to-all-done.8
  471.2 5.3 fusion.5
  476.5 4.7 fusion.7
  485.1 4.8 fusion.28
  491.9 3.0 fusion.33
  496.7 4.2 all-to-all-start.9
  509.2 4.2 all-to-all-start.11
  517.0 4.3 all-to-all-start.10
  521.6 3.3 all-to-all-done.10
  527.5 4.8 pad_maximum_fusion
  534.2 3.8 fusion.38
  538.9 39.4 %all-reduce.2 = (f32[1024]{0:T(1024)}, f32[1024]{0:T(1024)}) all-reduce(f32[1024]{0:T(1024)S(1)} %get-tuple-element.175, f32[1024]{0:T(1024)S(1)} %copy-done.44), channel_id=1, replica_groups=mesh['dp'=4,'blk'=2,'ulysses'=4] {'dp','blk','ulysses'}, use_global_device_ids=true, to_apply=%region_21.22 | all-reduce | flops 2048 | bytes 16384 | tf_op jit(solution)/shard_map/psum | solution.py:449
  578.3 109.9 %reduce-scatter.3.cloned.1.call-done = f32[32,3072]{1,0:T(8,128)} async-done(((f32[1024,3072]{1,0:T(8,128)}), f32[32,3072]{1,0:T(8,128)}) %reduce-scatter.3.cloned.1.call-update) | async-done | bytes 393232 | tf_op jit(solution)/shard_map/reduce_scatter | solution.py:424
  689.2 10.4 %all_gather.14 = bf16[128,3072]{1,0:T(8,128)(2,1)S(1)} all-gather(bf16[32,3072]{1,0:T(8,128)(2,1)S(1)} %convert_element_type.294), channel_id=1, replica_groups=mesh['dp'=4,'blk'=2,'ulysses'=4] {'ulysses'}, dimensions={0}, use_global_device_ids=true | all-gather | bytes 983040 | tf_op jit(solution)/shard_map/all_gather | solution.py:442
  701.5 35.3 %all-gather.8.cloned.1.call-done = bf16[3072,1024]{1,0:T(8,128)(2,1)} async-done(((bf16[768,1024]{1,0:T(8,128)(2,1)}), bf16[3072,1024]{1,0:T(8,128)(2,1)}) %all-gather.8.cloned.1.call-update) | async-done | bytes 6291472 | tf_op jit(solution)/shard_map/all_gather | solution.py:445
  736.8 6.8 slice.133
  746.1 115.6 %all-reduce.5.cloned.1.call-done = f32[1024,16]{0,1:T(8,128)} async-done(((f32[1024,16]{0,1:T(8,128)}), f32[1024,16]{0,1:T(8,128)}) %all-reduce.5.cloned.1.call-update) | async-done | bytes 65552 | tf_op jit(solution)/shard_map/psum | solution.py:449
  (287 shorter events, 95.2 us)
Async XLA Ops:
  7.2 276.1 %copy-start = (bf16[2,512,1024]{2,1,0:T(8,128)(2,1)S(1)}, bf16[2,512,1024]{2,1,0:T(8,128)(2,1)}, u32[]{:S(2)}) copy-start(bf16[2,512,1024]{2,1,0:T(8,128)(2,1)} %param.19) | copy-start | bytes 6291460
  7.2 77.3 %all-gather.4.cloned.1.call-start = ((), (), s32[]{:S(2)}) async-start(), calls=%async_computation.14 | async-start | bytes 4718592 | tf_op jit(solution)/shard_map/all_gather | solution.py:221
  7.9 131.3 %all-gather.6.cloned.1.call-start = ((), (), s32[]{:S(2)}) async-start(), calls=%async_computation.15 | async-start | bytes 2359296 | tf_op jit(solution)/shard_map/all_gather | solution.py:222
  11.5 76.8 %copy-start.49 = (f32[128]{0:T(128)}, f32[128]{0:T(128)S(1)}, u32[]{:S(2)}) copy-start(f32[128]{0:T(128)S(1)} %fusion.69) | copy-start | bytes 1540
  17.4 84.2 %copy-start.30 = (f32[128,32]{0,1:T(8,128)}, f32[128,32]{0,1:T(8,128)S(1)}, u32[]{:S(2)}) copy-start(f32[128,32]{0,1:T(8,128)S(1)} %get-tuple-element.206) | copy-start | bytes 49156
  17.4 84.2 %copy-start.32 = (f32[128,32]{0,1:T(8,128)}, f32[128,32]{0,1:T(8,128)S(1)}, u32[]{:S(2)}) copy-start(f32[128,32]{0,1:T(8,128)S(1)} %get-tuple-element.207) | copy-start | bytes 49156
  17.4 70.8 %copy-start.45 = (s32[1024,1]{0,1:T(1,128)}, s32[1024,1]{0,1:T(1,128)S(1)}, u32[]{:S(2)}) copy-start(s32[1024,1]{0,1:T(1,128)S(1)} %compare_select_fusion) | copy-start | bytes 12292
  88.5 9.2 %all-to-all-start = ((bf16[128,4,128]{2,0,1:T(8,128)(2,1)}), bf16[128,4,128]{2,0,1:T(8,128)(2,1)S(1)}, u32[]{:S(2)}, u32[]{:S(2)}) async-start(bf16[128,4,128]{2,0,1:T(8,128)(2,1)} %copy_bitcast_fusion.1), calls=%async_computation | async-start | bytes 262144 | tf_op jit(solution)/shard_map/all_to_all | solution.py:254
  97.7 7.5 all-to-all-start.1
  106.1 13.2 %collective-permute-start = (bf16[2,512,2,64]{1,3,2,0:T(8,128)(2,1)}, bf16[2,512,2,64]{1,3,2,0:T(8,128)(2,1)S(1)}, u32[]{:S(2)}, u32[]{:S(2)}) collective-permute-start(bf16[2,512,2,64]{1,3,2,0:T(8,128)(2,1)} %pad_maximum_fusion.4), channel_id=1, source_target_pairs={{0,4},{1,5},{2,6},{3,7},{8,12},{9,13},{10,14},{11,15},{16,20},{17,... | collective-permute-start | bytes 786440 | tf_op jit(solution)/shard_map/ppermute | solution.py:22
  109.4 9.6 %all-to-all-start.2 = ((bf16[128,4,256]{0,2,1:T(8,128)(2,1)}), bf16[128,4,256]{0,2,1:T(8,128)(2,1)S(1)}, u32[]{:S(2)}, u32[]{:S(2)}) async-start(bf16[128,4,256]{0,2,1:T(8,128)(2,1)} %bitcast.20), calls=%async_computation.2 | async-start | bytes 524288 | tf_op jit(solution)/shard_map/all_to_all | solution.py:252
  115.3 6.9 copy-start.26
  119.4 4.1 copy-start.25
  123.4 3.8 copy-start.43
  125.6 7.9 copy-start.41
  127.2 12.1 %copy-start.10 = (bf16[1,128,1024]{2,1,0:T(8,128)(2,1)S(1)}, bf16[1,128,1024]{2,1,0:T(8,128)(2,1)}, u32[]{:S(2)}) copy-start(bf16[1,128,1024]{2,1,0:T(8,128)(2,1)} %param.12) | copy-start | bytes 786436
  129.4 9.3 %all-to-all-start.3 = ((bf16[4,2,16384]{2,1,0:T(2,128)(2,1)}), bf16[4,2,16384]{2,1,0:T(2,128)(2,1)S(1)}, u32[]{:S(2)}, u32[]{:S(2)}) async-start(bf16[4,2,16384]{2,1,0:T(2,128)(2,1)} %reshape.608), calls=%async_computation.3 | async-start | bytes 524288 | tf_op jit(solution)/shard_map/all_to_all | solution.py:283
  139.2 9.8 %copy-start.15 = (bf16[128,4,1,256]{0,3,1,2:T(8,128)(2,1)}, bf16[128,4,1,256]{0,3,1,2:T(8,128)(2,1)S(1)}, u32[]{:S(2)}) copy-start(bf16[128,4,1,256]{0,3,1,2:T(8,128)(2,1)S(1)} %copy.213) | copy-start | bytes 786436
  139.2 4.7 copy-start.40
  141.9 7.1 copy-start.53
  149.0 6.0 copy-start.13
  149.0 7.0 copy-start.38
  149.0 8.3 copy-start.46
  149.0 63.7 %all-to-all-start.4 = ((bf16[16,80,1024]{2,1,0:T(8,128)(2,1)}), bf16[16,80,1024]{2,1,0:T(8,128)(2,1)}, u32[]{:S(2)}, u32[]{:S(2)}) async-start(bf16[16,80,1024]{2,1,0:T(8,128)(2,1)} %bitcast.250), calls=%async_computation.4 | async-start | bytes 5242880 | tf_op jit(solution)/shard_map/all_to_all | solution.py:320
  212.7 62.8 %all-to-all-start.6 = ((bf16[16,80,1024]{2,1,0:T(8,128)(2,1)}), bf16[16,80,1024]{2,1,0:T(8,128)(2,1)}, u32[]{:S(2)}, u32[]{:S(2)}) async-start(bf16[16,80,1024]{2,1,0:T(8,128)(2,1)} %bitcast.249), calls=%async_computation.6 | async-start | bytes 5242880 | tf_op jit(solution)/shard_map/all_to_all | solution.py:321
  277.7 5.6 copy-start.6
  283.3 3.7 copy-start.59
  294.4 63.6 %all-to-all-start.7 = ((bf16[2,640,1024]{2,0,1:T(2,128)(2,1)}), bf16[2,640,1024]{2,0,1:T(2,128)(2,1)}, u32[]{:S(2)}, u32[]{:S(2)}) async-start(bf16[2,640,1024]{2,0,1:T(2,128)(2,1)} %copy.227), calls=%async_computation.7 | async-start | bytes 5242880 | tf_op jit(solution)/shard_map/all_to_all | solution.py:330
  302.6 4.3 copy-start.8
  302.6 4.2 copy-start.21
  309.1 6.5 copy-start.19
  357.9 63.4 %all-to-all-start.5 = ((bf16[2,640,1024]{2,0,1:T(2,128)(2,1)}), bf16[2,640,1024]{2,0,1:T(2,128)(2,1)}, u32[]{:S(2)}, u32[]{:S(2)}) async-start(bf16[2,640,1024]{2,0,1:T(2,128)(2,1)} %copy.221), calls=%async_computation.5 | async-start | bytes 5242880 | tf_op jit(solution)/shard_map/all_to_all | solution.py:327
  363.1 169.3 %reduce-scatter.5.cloned.1.call-start = ((), (), s32[]{:S(2)}) async-start(), calls=%async_computation.18 | async-start | bytes 7864320 | tf_op jit(solution)/shard_map/reduce_scatter | solution.py:435
  445.0 4.7 copy-start.48
  445.0 4.7 copy-start.52
  445.0 8.2 copy-start.39
  449.6 3.6 copy-start.35
  449.6 3.6 copy-start.54
  449.6 4.7 copy-start.58
  449.6 4.7 copy-start.22
  449.7 4.7 copy-start.17
  449.8 6.1 copy-start.36
  449.8 6.1 copy-start.9
  457.0 13.9 %all-to-all-start.8 = ((bf16[128,4,256]{2,0,1:T(8,128)(2,1)}), bf16[128,4,256]{2,0,1:T(8,128)(2,1)S(1)}, u32[]{:S(2)}, u32[]{:S(2)}) async-start(bf16[128,4,256]{2,0,1:T(8,128)(2,1)} %bitcast.234), calls=%async_computation.8 | async-start | bytes 524288 | tf_op jit(solution)/shard_map/all_to_all | solution.py:366
  476.5 6.7 copy-start.24
  485.0 6.9 copy-start.27
  485.0 6.9 copy-start.29
  490.4 10.4 %copy-start.16 = (bf16[128,4,1,256]{0,3,1,2:T(8,128)(2,1)S(1)}, bf16[128,4,1,256]{0,3,1,2:T(8,128)(2,1)}, u32[]{:S(2)}) copy-start(bf16[128,4,1,256]{0,3,1,2:T(8,128)(2,1)} %copy-done.15) | copy-start | bytes 786436
  490.6 16.0 %collective-permute-start.1 = (bf16[2,512,2,64]{1,3,2,0:T(8,128)(2,1)S(1)}, bf16[2,512,2,64]{1,3,2,0:T(8,128)(2,1)}, u32[]{:S(2)}, u32[]{:S(2)}) collective-permute-start(bf16[2,512,2,64]{1,3,2,0:T(8,128)(2,1)S(1)} %fusion.47), channel_id=1, source_target_pairs={{4,0},{5,1},{6,2},{7,3},{12,8},{13,9},{14,10},{15,11},{20,16},{21,... | collective-permute-start | bytes 786440 | tf_op jit(solution)/shard_map/ppermute | solution.py:22
  496.7 9.4 %all-to-all-start.9 = ((bf16[4,2,16384]{2,1,0:T(2,128)(2,1)}), bf16[4,2,16384]{2,1,0:T(2,128)(2,1)S(1)}, u32[]{:S(2)}, u32[]{:S(2)}) async-start(bf16[4,2,16384]{2,1,0:T(2,128)(2,1)} %reshape.614), calls=%async_computation.9 | async-start | bytes 524288 | tf_op jit(solution)/shard_map/all_to_all | solution.py:384
  503.6 9.8 %copy-start.31 = (f32[128,32]{0,1:T(8,128)S(1)}, f32[128,32]{0,1:T(8,128)}, u32[]{:S(2)}) copy-start(f32[128,32]{0,1:T(8,128)} %copy-done.30) | copy-start | bytes 49156
  503.6 9.8 %copy-start.33 = (f32[128,32]{0,1:T(8,128)S(1)}, f32[128,32]{0,1:T(8,128)}, u32[]{:S(2)}) copy-start(f32[128,32]{0,1:T(8,128)} %copy-done.32) | copy-start | bytes 49156
  506.6 18.7 %copy-start.11 = (bf16[1,128,1024]{2,1,0:T(8,128)(2,1)S(1)}, bf16[1,128,1024]{2,1,0:T(8,128)(2,1)}, u32[]{:S(2)}) copy-start(bf16[1,128,1024]{2,1,0:T(8,128)(2,1)} %param.12) | copy-start | bytes 786436
  506.6 18.7 %copy-start.34 = (f32[1024]{0:T(1024)S(1)}, f32[1024]{0:T(1024)}, u32[]{:S(2)}) copy-start(f32[1024]{0:T(1024)} %param.13) | copy-start | bytes 12292
  506.6 18.7 %copy-start.50 = (f32[128]{0:T(128)S(1)}, f32[128]{0:T(128)}, u32[]{:S(2)}) copy-start(f32[128]{0:T(128)} %copy-done.49) | copy-start | bytes 1540
  509.2 7.8 all-to-all-start.11
  517.0 7.9 all-to-all-start.10
  521.3 166.9 %reduce-scatter.3.cloned.1.call-start = ((), (), s32[]{:S(2)}) async-start(), calls=%async_computation.16 | async-start | bytes 12976128 | tf_op jit(solution)/shard_map/reduce_scatter | solution.py:424
  532.4 5.6 copy-start.56
  532.4 204.5 %all-gather.8.cloned.1.call-start = ((), (), s32[]{:S(2)}) async-start(), calls=%async_computation.19 | async-start | bytes 7864320 | tf_op jit(solution)/shard_map/all_gather | solution.py:445
  533.0 5.9 copy-start.44
  533.0 328.7 %all-reduce.5.cloned.1.call-start = ((), (), s32[]{:S(2)}) async-start(), calls=%async_computation.17 | async-start | bytes 131072 | tf_op jit(solution)/shard_map/psum | solution.py:449
  736.8 6.8 copy-start.4
  736.8 126.4 %copy-start.1 = (bf16[2,512,1024]{2,1,0:T(8,128)(2,1)S(1)}, bf16[2,512,1024]{2,1,0:T(8,128)(2,1)}, u32[]{:S(2)}) copy-start(bf16[2,512,1024]{2,1,0:T(8,128)(2,1)} %param.19) | copy-start | bytes 6291460
  (16 other events, 30.3 us)
Sparse Core Ops, SparseCore 0:
  10.2 74.2 all-gather.3
  86.6 47.6 all-gather.5
  412.4 62.4 reduce-scatter.4
  532.5 155.6 reduce-scatter.2
  689.6 47.1 all-gather.7
  742.9 118.8 all-reduce.4
where the time goes:
time: 881 us; the launch traced here: 870 us
  waiting for transfers between devices  494 us (56%)
  local copies, waits for them, and re-layouts  98.4 us (11%)
  matrix products  84.4 us (10%)
  starting transfers between devices  60.3 us (7%)
  other arithmetic  60 us (7%)
  blocking collectives  49.8 us (6%)
  between operations  15.8 us (2%)
    psum x1, waiting for transfers between devices, body(): lax.psum((gain_attn_grad, gain_mix_grad, router_grad), ('dp', 'blk', 'uly...  116 us
    reduce_scatter x1, waiting for transfers between devices, body(): lax.psum_scatter(jnp.concatenate([qkv_term, out_term], axis=1), ('dp', 'b...  110 us
    all_gather x1, waiting for transfers between devices, body(): lax.all_gather(query_key_value_weight, ('dp', 'blk'), axis=0, tiled=True)  62.1 us
    all_to_all x1, waiting for transfers between devices, body(): lax.all_to_all(expert_grad, ('dp', 'blk'), split_axis=0, concat_axis=1, t...  54.7 us
    all_to_all x1, waiting for transfers between devices, body(): lax.all_to_all(dispatched, ('dp', 'blk'), split_axis=0, concat_axis=1, ti...  42.9 us
    psum x1, blocking collectives, body(): lax.psum((gain_attn_grad, gain_mix_grad, router_grad), ('dp', 'blk', 'uly...  39.4 us
    all_to_all x1, waiting for transfers between devices, body(): lax.all_to_all(held_row_grads.astype(jnp.bfloat16), ('dp', 'blk'), split_...  37.1 us
    all_gather x1, waiting for transfers between devices, body(): lax.all_gather(expert_part.astype(jnp.bfloat16), 'ulysses', axis=0, tiled...  35.3 us
  transfers between devices with their start and end apart: 20, of which 16 were waited for; matrix products, arithmetic and copies ran while one was open for 24% of the time, Pallas kernels for 0%

commit v1 on v0

v1 whole, which is shorter than its diff:
```python
import functools
import math

import jax
import jax.numpy as jnp
from jax import lax
from jax.experimental import pallas as pl
from jax.experimental.pallas import tpu as pltpu
from jax.sharding import PartitionSpec as P

QUERY_HEADS = 16
KEY_VALUE_HEADS = 8
HEAD_SIZE = 64
CAPACITY = 80


EPSILON = 1e-06
THETA = 10000.0
MASKED = -1e30


def passed_along(value, axis, steps):
    count = lax.axis_size(axis)
    initial, last = (max(0, -steps), min(count, count - steps))
    return lax.ppermute(value, axis, [(source, source + steps) for source in range(initial, last)])


def rms_scale(values, gain):
    return values * lax.rsqrt(jnp.mean(values * values, axis=-1, keepdims=True) + EPSILON) * gain


def rotary_tables(positions, head_width):
    exponent = jnp.arange(head_width // 2, dtype=jnp.float32) * (2.0 / head_width)
    inverse = jnp.exp(-math.log(THETA) * exponent)
    angles = positions.astype(jnp.float32)[:, None] * inverse[None, :]
    return (jnp.cos(angles)[:, None, :], jnp.sin(angles)[:, None, :])


def rotate(values, cosine, sine):
    half_size = values.shape[-1] // 2
    first_half = values[..., :half_size]
    second_half = values[..., half_size:]
    return jnp.concatenate(
        [first_half * cosine - second_half * sine, second_half * cosine + first_half * sine],
        axis=-1,
    )


def rotate_back(grad_values, cosine, sine):
    half_size = grad_values.shape[-1] // 2
    first_half = grad_values[..., :half_size]
    second_half = grad_values[..., half_size:]
    return jnp.concatenate(
        [first_half * cosine + second_half * sine, second_half * cosine - first_half * sine],
        axis=-1,
    )


def attend_forward(queries, all_keys, all_values, query_pos, key_pos, key_ok, row_block):
    score_scale = queries.shape[-1] ** (-0.5)
    block_count = queries.shape[0] // row_block

    def one_block(block_index):
        offset = block_index * row_block
        row_part = lax.dynamic_slice_in_dim(queries, offset, row_block, 0)
        query_here = lax.dynamic_slice_in_dim(query_pos, offset, row_block, 0)
        scores = (
            jnp.einsum("qrgd,krd->qrgk", row_part, all_keys, preferred_element_type=jnp.float32)
            * score_scale
        )
        allowed = (key_pos[None, :] <= query_here[:, None]) & key_ok[None, :]
        scores = jnp.where(allowed[:, None, None, :], scores, MASKED)
        row_peak = jnp.max(scores, axis=-1, keepdims=True)
        exps_all = jnp.exp(scores - row_peak)
        row_total = jnp.sum(exps_all, axis=-1, keepdims=True)
        weights_low = (exps_all / row_total).astype(jnp.bfloat16)
        mixed_part = jnp.einsum(
            "qrgk,krd->qrgd", weights_low, all_values, preferred_element_type=jnp.float32
        )
        return (mixed_part, (row_peak + jnp.log(row_total))[..., 0])

    mixed_blocks, log_sums = lax.map(one_block, jnp.arange(block_count, dtype=jnp.int32))
    return (mixed_blocks.reshape(queries.shape), log_sums.reshape(queries.shape[:3]))


def attend_backward(
    queries, all_keys, all_values, query_pos, key_pos, key_ok, log_sums, mixed_grad, row_block
):
    score_scale = queries.shape[-1] ** (-0.5)
    block_count = queries.shape[0] // row_block

    def one_block(carry, block_index):
        key_grads, value_grads = carry
        offset = block_index * row_block
        row_part = lax.dynamic_slice_in_dim(queries, offset, row_block, 0)
        query_here = lax.dynamic_slice_in_dim(query_pos, offset, row_block, 0)
        grad_part = lax.dynamic_slice_in_dim(mixed_grad, offset, row_block, 0)
        sums_part = lax.dynamic_slice_in_dim(log_sums, offset, row_block, 0)
        scores = (
            jnp.einsum("qrgd,krd->qrgk", row_part, all_keys, preferred_element_type=jnp.float32)
            * score_scale
        )
        allowed = (key_pos[None, :] <= query_here[:, None]) & key_ok[None, :]
        scores = jnp.where(allowed[:, None, None, :], scores, MASKED)
        probs_all = jnp.exp(scores - sums_part[..., None])
        value_grads = value_grads + jnp.einsum(
            "qrgk,qrgd->krd",
            probs_all.astype(jnp.bfloat16),
            grad_part,
            preferred_element_type=jnp.float32,
        )
        probs_grad = jnp.einsum(
            "qrgd,krd->qrgk", grad_part, all_values, preferred_element_type=jnp.float32
        )
        score_grad = probs_all * (
            probs_grad - jnp.sum(probs_all * probs_grad, axis=-1, keepdims=True)
        )
        score_low = score_grad.astype(jnp.bfloat16)
        row_grads = (
            jnp.einsum("qrgk,krd->qrgd", score_low, all_keys, preferred_element_type=jnp.float32)
            * score_scale
        )
        key_grads = (
            key_grads
            + jnp.einsum("qrgk,qrgd->krd", score_low, row_part, preferred_element_type=jnp.float32)
            * score_scale
        )
        return ((key_grads, value_grads), row_grads)

    zero_grads = jnp.zeros(all_keys.shape, jnp.float32)
    (key_grads, value_grads), row_grads = lax.scan(
        one_block, (zero_grads, zero_grads), jnp.arange(block_count, dtype=jnp.int32)
    )
    return (row_grads.reshape(queries.shape), key_grads, value_grads)


MESH = pl.DeviceIdType.MESH
TOKEN_AXES = ("ulysses",)
EXPERT_AXES = ("dp", "blk")
VMEM_LIMIT = 40 * 1024 * 1024


def flat_index(axes, sizes):
    index = lax.axis_index(axes[0])
    for axis, size in zip(axes[1:], sizes[1:]):
        index = index * size + lax.axis_index(axis)
    return index


def device_of(axes, sizes, index):
    place = {}
    for axis, size in zip(reversed(axes), reversed(sizes)):
        place[axis] = lax.rem(index, size)
        index = index // size
    return place


def greet(places):
    barrier = pltpu.get_barrier_semaphore()
    for place in places:
        pl.semaphore_signal(barrier, inc=1, device_id=place, device_id_type=MESH)
    pl.semaphore_wait(barrier, len(places))


def remote(source, target, send, recv, place):
    return pltpu.make_async_remote_copy(
        src_ref=source,
        dst_ref=target,
        send_sem=send,
        recv_sem=recv,
        device_id=place,
        device_id_type=MESH,
    )


def direct_copies(axes, sizes, personal, ins, outs, send, recv, local):
    count = math.prod(sizes)
    me = flat_index(axes, sizes)
    copies = []
    for step in range(1, count):
        other = lax.rem(me + step, count)
        place = device_of(axes, sizes, other)
        for item, (source, target) in enumerate(zip(ins, outs)):
            copies.append(
                remote(
                    source.at[other] if personal[item] else source,
                    target.at[me],
                    send.at[item, step],
                    recv.at[item, step],
                    place,
                )
            )
    for item, (source, target) in enumerate(zip(ins, outs)):
        copies.append(
            pltpu.make_async_copy(
                source.at[me] if personal[item] else source, target.at[me], local.at[item]
            )
        )
    return copies


def other_places(axes, sizes):
    count = math.prod(sizes)
    me = flat_index(axes, sizes)
    return [device_of(axes, sizes, lax.rem(me + step, count)) for step in range(1, count)]


def exchange_kernel(axes, sizes, personal, *refs):
    count = len(personal)
    ins, outs = refs[:count], refs[count : 2 * count]
    send, recv, local = refs[2 * count :]
    greet(other_places(axes, sizes))
    copies = direct_copies(axes, sizes, personal, ins, outs, send, recv, local)
    for copy in copies:
        copy.start()
    for copy in copies:
        copy.wait()


def exchange(values, personal, axes, sizes, collective_id):
    count = math.prod(sizes)
    shapes = [
        jax.ShapeDtypeStruct(value.shape if one else (count,) + value.shape, value.dtype)
        for value, one in zip(values, personal)
    ]
    total = len(values)
    return pl.pallas_call(
        functools.partial(exchange_kernel, axes, sizes, personal),
        out_shape=shapes,
        in_specs=[pl.BlockSpec(memory_space=pl.ANY)] * total,
        out_specs=[pl.BlockSpec(memory_space=pl.ANY)] * total,
        scratch_shapes=[
            pltpu.SemaphoreType.DMA((total, count)),
            pltpu.SemaphoreType.DMA((total, count)),
            pltpu.SemaphoreType.DMA((total,)),
        ],
        compiler_params=pltpu.CompilerParams(collective_id=collective_id, has_side_effects=True),
    )(*values)


def gather_kernel(sizes, token_sizes, wide, near, *refs):
    total = wide + near
    ins, outs = refs[:total], refs[total : 2 * total]
    line_send, line_recv, side_send, side_recv, local, near_send, near_recv, near_local = refs[
        2 * total :
    ]
    line, pair = sizes
    here, side = lax.axis_index("dp"), lax.axis_index("blk")
    me = here * pair + side
    across = {"blk": 1 - side}
    places = [{"dp": lax.rem(here + step, line)} for step in range(1, line)]
    greet(places + [across] + (other_places(TOKEN_AXES, token_sizes) if near else []))
    waits = []
    for item in range(wide):
        for step in range(line - 1, 0, -1):
            copy = remote(
                ins[item],
                outs[item].at[me],
                line_send.at[item, step],
                line_recv.at[item, step],
                places[step - 1],
            )
            copy.start()
        copy = remote(
            ins[item], outs[item].at[me], side_send.at[item, 0], side_recv.at[item, 0], across
        )
        copy.start()
        waits.append(copy)
        copy = pltpu.make_async_copy(ins[item], outs[item].at[me], local.at[item])
        copy.start()
        waits.append(copy)
    if near:
        for copy in direct_copies(
            TOKEN_AXES,
            token_sizes,
            (False,) * near,
            ins[wide:],
            outs[wide:],
            near_send,
            near_recv,
            near_local,
        ):
            copy.start()
            waits.append(copy)
    for step in range(1, line):
        for item in range(wide):
            arrived = remote(
                ins[item],
                outs[item].at[me],
                line_send.at[item, step],
                line_recv.at[item, step],
                places[step - 1],
            )
            arrived.wait()
            block = lax.rem(here + line - step, line) * pair + side
            copy = remote(
                outs[item].at[block],
                outs[item].at[block],
                side_send.at[item, step],
                side_recv.at[item, step],
                across,
            )
            copy.start()
            waits.append(copy)
    for copy in waits:
        copy.wait()


def gather_wide(values, near_values, sizes, token_sizes, collective_id):
    count = math.prod(sizes)
    near_count = math.prod(token_sizes)
    wide, near = len(values), len(near_values)
    shapes = [jax.ShapeDtypeStruct((count,) + value.shape, value.dtype) for value in values]
    shapes += [
        jax.ShapeDtypeStruct((near_count,) + value.shape, value.dtype) for value in near_values
    ]
    return pl.pallas_call(
        functools.partial(gather_kernel, sizes, token_sizes, wide, near),
        out_shape=shapes,
        in_specs=[pl.BlockSpec(memory_space=pl.ANY)] * (wide + near),
        out_specs=[pl.BlockSpec(memory_space=pl.ANY)] * (wide + near),
        scratch_shapes=[
            pltpu.SemaphoreType.DMA((wide, sizes[0])),
            pltpu.SemaphoreType.DMA((wide, sizes[0])),
            pltpu.SemaphoreType.DMA((wide, sizes[0])),
            pltpu.SemaphoreType.DMA((wide, sizes[0])),
            pltpu.SemaphoreType.DMA((wide,)),
            pltpu.SemaphoreType.DMA((max(near, 1), near_count)),
            pltpu.SemaphoreType.DMA((max(near, 1), near_count)),
            pltpu.SemaphoreType.DMA((max(near, 1),)),
        ],
        compiler_params=pltpu.CompilerParams(collective_id=collective_id, has_side_effects=True),
    )(*values, *near_values)


def reduce_kernel(sizes, total, personal, *refs):
    small = len(personal)
    ins, refs = refs[:total], refs[total:]
    small_ins, refs = refs[:small], refs[small:]
    outs, refs = refs[:total], refs[total:]
    small_outs, refs = refs[:small], refs[small:]
    side_bufs, refs = refs[:total], refs[total:]
    sent_bufs, refs = refs[:total], refs[total:]
    line_bufs, refs = refs[:total], refs[total:]
    side_send, side_recv, line_send, line_recv, send, recv, local = refs
    line, pair = sizes
    here, side = lax.axis_index("dp"), lax.axis_index("blk")
    across = {"blk": 1 - side}
    greet(other_places(EXPERT_AXES, sizes))

    def side_copy(item, step):
        target = lax.rem(here + step, line)
        return remote(
            ins[item].at[target * pair + 1 - side],
            side_bufs[item].at[step],
            side_send.at[item, step],
            side_recv.at[item, step],
            across,
        )

    def line_copy(item, step):
        return remote(
            sent_bufs[item].at[step],
            line_bufs[item].at[step],
            line_send.at[item, step],
            line_recv.at[item, step],
            {"dp": lax.rem(here + step, line)},
        )

    order = list(range(1, line)) + [0]
    for step in order:
        for item in range(total):
            side_copy(item, step).start()
    copies = direct_copies(
        EXPERT_AXES, sizes, personal, small_ins, small_outs, send, recv, local
    )
    for copy in copies:
        copy.start()
    for step in order:
        for item in range(total):
            side_copy(item, step).wait()
            block = lax.rem(here + step, line) * pair + side
            both = ins[item][block].astype(jnp.float32) + side_bufs[item][step].astype(jnp.float32)
            if step:
                sent_bufs[item][step] = both.astype(jnp.bfloat16)
                line_copy(item, step).start()
            else:
                outs[item][...] = both
    for step in range(1, line):
        for item in range(total):
            line_copy(item, step).wait()
            outs[item][...] += line_bufs[item][step].astype(jnp.float32)
    for copy in copies:
        copy.wait()


def reduce_wide(values, small_values, personal, sizes, collective_id):
    count = math.prod(sizes)
    total, small = len(values), len(small_values)
    shapes = [jax.ShapeDtypeStruct(value.shape[1:], jnp.float32) for value in values]
    shapes += [
        jax.ShapeDtypeStruct(value.shape if one else (count,) + value.shape, value.dtype)
        for value, one in zip(small_values, personal)
    ]
    buffers = [pltpu.VMEM((sizes[0],) + value.shape[1:], jnp.bfloat16) for value in values]
    wide_sems = pltpu.SemaphoreType.DMA((total, sizes[0]))
    return pl.pallas_call(
        functools.partial(reduce_kernel, sizes, total, personal),
        out_shape=shapes,
        in_specs=[pl.BlockSpec(memory_space=pltpu.VMEM)] * (total + small),
        out_specs=[pl.BlockSpec(memory_space=pltpu.VMEM)] * (total + small),
        scratch_shapes=buffers * 3
        + [wide_sems] * 4
        + [
            pltpu.SemaphoreType.DMA((small, count)),
            pltpu.SemaphoreType.DMA((small, count)),
            pltpu.SemaphoreType.DMA((small,)),
        ],
        compiler_params=pltpu.CompilerParams(
            collective_id=collective_id, has_side_effects=True, vmem_limit_bytes=VMEM_LIMIT
        ),
    )(*values, *small_values)


def dense_gates(logits, mask):
    masked = jnp.where(mask, logits, MASKED)
    exps = jnp.where(mask, jnp.exp(masked - jnp.max(masked, axis=-1, keepdims=True)), 0.0)
    return exps / jnp.sum(exps, axis=-1, keepdims=True)


def body(
    inputs,
    gain_attn,
    query_key_value_weight,
    w_out,
    gain_mix,
    router,
    expert_in,
    expert_down,
    routes,
    cotangent,
):
    cycle_size = lax.axis_size("blk")
    slice_total = lax.axis_size("ulysses")
    sizes = (lax.axis_size("dp"), cycle_size)
    token_sizes = (slice_total,)
    groups = math.prod(sizes)
    cycle_index = lax.axis_index("blk")
    slice_index = lax.axis_index("ulysses")
    token_rows = inputs.shape[1]
    width = inputs.shape[2]
    head_width = HEAD_SIZE
    head_copies = max(1, slice_total // KEY_VALUE_HEADS)
    repeated_heads = KEY_VALUE_HEADS * head_copies
    group_size = QUERY_HEADS // repeated_heads
    local_rep = repeated_heads // slice_total
    local_query = QUERY_HEADS // slice_total
    span_len = token_rows * slice_total
    row_block = min(512, span_len)
    query_columns = QUERY_HEADS * head_width
    key_value_columns = KEY_VALUE_HEADS * head_width
    query_part = local_query * head_width
    pair_part = local_rep * head_width
    num_experts = router.shape[1]
    held = expert_in.shape[0]
    hidden_units = expert_down.shape[1]
    bf16 = jnp.bfloat16
    f32 = jnp.float32

    layer_in = inputs[0].astype(f32)
    norm_attn = rms_scale(layer_in, gain_attn).astype(bf16)
    mask = jnp.any(
        routes[0][:, :, None] == jnp.arange(num_experts, dtype=jnp.int32)[None, None, :], axis=1
    )
    query_start = slice_index * query_part
    pair_start = (slice_index * local_rep) // head_copies * head_width
    weight_part = jnp.concatenate(
        [
            lax.dynamic_slice_in_dim(query_key_value_weight, query_start, query_part, 1),
            lax.dynamic_slice_in_dim(
                query_key_value_weight, query_columns + pair_start, pair_part, 1
            ),
            lax.dynamic_slice_in_dim(
                query_key_value_weight,
                query_columns + key_value_columns + pair_start,
                pair_part,
                1,
            ),
            lax.dynamic_slice_in_dim(w_out, query_start, query_part, 1),
        ],
        axis=1,
    )
    weight_blocks, mask_blocks, norm_blocks = gather_wide(
        [weight_part, mask.astype(bf16).T], [norm_attn], sizes, token_sizes, 0
    )
    held_cotangent = lax.all_gather(cotangent[0], EXPERT_AXES, axis=0, tiled=True)
    weights = weight_blocks.reshape(width, -1)
    own_columns = query_part + 2 * pair_part
    qkv_weight = weights[:, :own_columns]
    out_weight = weights[:, own_columns:]
    span_norm = norm_blocks.reshape(span_len, width)
    projected = jnp.dot(span_norm, qkv_weight, preferred_element_type=f32)
    span_rows = jnp.arange(span_len, dtype=jnp.int32)
    query_pos = cycle_index * span_len + span_rows
    cosine, sine = rotary_tables(query_pos, head_width)
    q_raw = projected[:, :query_part].reshape(span_len, local_query, head_width)
    key_plain = projected[:, query_part : query_part + pair_part].reshape(
        span_len, local_rep, head_width
    )
    value_plain = projected[:, query_part + pair_part :].reshape(span_len, local_rep, head_width)
    queries = (
        rotate(q_raw, cosine, sine)
        .astype(bf16)
        .reshape(span_len, local_rep, group_size, head_width)
    )
    own_pair = jnp.stack([rotate(key_plain, cosine, sine).astype(bf16), value_plain.astype(bf16)])
    earlier_pair = passed_along(own_pair, "blk", 1)
    all_keys = jnp.concatenate([own_pair[0], earlier_pair[0]], axis=0)
    all_values = jnp.concatenate([own_pair[1], earlier_pair[1]], axis=0)
    key_pos = jnp.concatenate(
        [(cycle_index - cycle_step) * span_len + span_rows for cycle_step in range(cycle_size)]
    )
    key_ok = jnp.concatenate(
        [
            jnp.broadcast_to(cycle_index - cycle_step >= 0, (span_len,))
            for cycle_step in range(cycle_size)
        ]
    )
    attn_heads, log_sums = attend_forward(
        queries, all_keys, all_values, query_pos, key_pos, key_ok, row_block
    )
    mixed = attn_heads.astype(bf16).reshape(span_len, query_part)
    branch_part = lax.dot_general(
        mixed, out_weight, (((1,), (1,)), ((), ())), preferred_element_type=f32
    )
    (branch_blocks,) = exchange(
        [branch_part.astype(bf16).reshape(slice_total, token_rows, width)],
        (True,),
        TOKEN_AXES,
        token_sizes,
        1,
    )
    residual = layer_in + jnp.sum(branch_blocks.astype(f32), axis=0)
    norm_mix = rms_scale(residual, gain_mix).astype(bf16)
    (mix_blocks,) = gather_wide([norm_mix], [], sizes, token_sizes, 2)

    rows = mix_blocks.reshape(groups * token_rows, width)
    row_mask = jnp.swapaxes(mask_blocks, 1, 2).reshape(groups * token_rows, num_experts) > 0
    row_gates = dense_gates(jnp.dot(rows, router, preferred_element_type=f32), row_mask)
    first_held = flat_index(EXPERT_AXES, sizes) * held
    own_gates = lax.dynamic_slice_in_dim(row_gates, first_held, held, 1)
    row_grad = held_cotangent.astype(f32)
    combined = 0.0
    gate_grads, both_list, in_terms, down_terms = [], [], [], []
    for expert in range(held):
        weight_in, weight_down = expert_in[expert], expert_down[expert]
        gate = own_gates[:, expert : expert + 1]
        both_halves = jnp.dot(rows, weight_in, preferred_element_type=f32)
        gate_half = both_halves[:, :hidden_units]
        up_half = both_halves[:, hidden_units:]
        sigmoid_gate = jax.nn.sigmoid(gate_half)
        activated = gate_half * sigmoid_gate
        hidden = (activated * up_half).astype(bf16)
        expert_out = jnp.dot(hidden, weight_down, preferred_element_type=f32)
        combined = combined + gate * expert_out
        gate_grads.append(jnp.sum(row_grad * expert_out, axis=-1))
        expert_grad = (gate * row_grad).astype(bf16)
        hidden_grad = lax.dot_general(
            expert_grad, weight_down, (((1,), (1,)), ((), ())), preferred_element_type=f32
        )
        gate_half_grad = (
            hidden_grad * up_half * sigmoid_gate * (1.0 + gate_half * (1.0 - sigmoid_gate))
        )
        both_grad = jnp.concatenate([gate_half_grad, hidden_grad * activated], axis=-1).astype(
            bf16
        )
        both_list.append(both_grad)
        in_terms.append((rows, both_grad))
        down_terms.append((hidden, expert_grad))
    dispatch_sum = sum(
        lax.dot_general(
            both_list[expert],
            expert_in[expert],
            (((1,), (1,)), ((), ())),
            preferred_element_type=f32,
        )
        for expert in range(held)
    )

    def weight_term(pairs):
        return jnp.concatenate(
            [
                lax.dot_general(
                    left, right, (((0,), (0,)), ((), ())), preferred_element_type=f32
                ).astype(bf16)
                for left, right in pairs
            ],
            axis=0,
        )

    gate_rows = jnp.stack(gate_grads + [jnp.zeros_like(gate_grads[0])] * (-held % 8))
    gate_send = jnp.swapaxes(gate_rows.reshape(-1, groups, token_rows), 0, 1)
    combined_sum, mix_grad, gate_blocks = reduce_wide(
        [
            combined.astype(bf16).reshape(groups, token_rows, width),
            dispatch_sum.astype(bf16).reshape(groups, token_rows, width),
        ],
        [gate_send],
        (True,),
        sizes,
        3,
    )
    in_part = lax.psum_scatter(
        weight_term(in_terms), "ulysses", scatter_dimension=0, tiled=True
    )
    down_part = lax.psum_scatter(
        weight_term(down_terms), "ulysses", scatter_dimension=0, tiled=True
    )
    grad_expert_in = (
        lax.all_gather(in_part, "ulysses", axis=0, tiled=True)
        .astype(f32)
        .reshape(expert_in.shape)
    )
    grad_expert_down = (
        lax.all_gather(down_part, "ulysses", axis=0, tiled=True)
        .astype(f32)
        .reshape(expert_down.shape)
    )

    result = (residual + combined_sum).astype(bf16)
    out_grad = cotangent[0].astype(f32)
    gate_values = dense_gates(jnp.dot(norm_mix, router, preferred_element_type=f32), mask)
    gate_grad = gate_blocks[:, :held, :].reshape(num_experts, token_rows).T
    logit_grad = gate_values * (
        gate_grad - jnp.sum(gate_values * gate_grad, axis=-1, keepdims=True)
    )
    mix_grad = mix_grad + jnp.dot(
        logit_grad, router.astype(f32).T, precision=lax.Precision.HIGHEST
    )
    router_grad = jnp.dot(
        logit_grad.T, norm_mix.astype(f32), precision=lax.Precision.HIGHEST
    )
    _, mix_back = jax.vjp(rms_scale, residual, gain_mix)
    residual_norm_grad, gain_mix_grad = mix_back(mix_grad)
    residual_grad = out_grad + residual_norm_grad
    branch_grad = residual_grad.astype(bf16)
    shared = jnp.concatenate([router_grad, gain_mix_grad[None]], axis=0)
    shared = jnp.pad(shared, ((0, -shared.shape[0] % 8), (0, 0)))
    shared_rows = shared.shape[0]
    shared_send = jnp.swapaxes(shared.reshape(shared_rows, slice_total, -1), 0, 1)
    grad_blocks, shared_blocks = exchange(
        [branch_grad, shared_send], (False, True), TOKEN_AXES, token_sizes, 4
    )
    span_grad = grad_blocks.reshape(span_len, width)
    shared_part = jnp.sum(shared_blocks, axis=0)
    mixed_grad = (
        jnp.dot(span_grad, out_weight, preferred_element_type=f32)
        .astype(bf16)
        .reshape(span_len, local_rep, group_size, head_width)
    )
    query_grad, key_grads, value_grads = attend_backward(
        queries, all_keys, all_values, query_pos, key_pos, key_ok, log_sums, mixed_grad, row_block
    )
    pair_grads = jnp.stack([key_grads, value_grads]).reshape(
        2, cycle_size, span_len, local_rep, head_width
    )
    own_grads = pair_grads[:, 0] + passed_along(
        pair_grads[:, 1].astype(bf16), "blk", -1
    ).astype(f32)
    own_grads = own_grads.astype(bf16).astype(f32)
    dq_raw = rotate_back(
        query_grad.astype(bf16).astype(f32).reshape(span_len, local_query, head_width),
        cosine,
        sine,
    )
    dk_raw = rotate_back(own_grads[0], cosine, sine)
    qkv_grad = jnp.concatenate(
        [
            dq_raw.reshape(span_len, query_part),
            dk_raw.reshape(span_len, pair_part),
            own_grads[1].reshape(span_len, pair_part),
        ],
        axis=1,
    ).astype(bf16)
    norm_grad_part = lax.dot_general(
        qkv_grad, qkv_weight, (((1,), (1,)), ((), ())), preferred_element_type=f32
    )
    (norm_grad_blocks,) = exchange(
        [norm_grad_part.astype(bf16).reshape(slice_total, token_rows, width)],
        (True,),
        TOKEN_AXES,
        token_sizes,
        5,
    )
    attn_norm_grad = jnp.sum(norm_grad_blocks.astype(f32), axis=0)
    _, attn_back = jax.vjp(rms_scale, layer_in, gain_attn)
    input_norm_grad, gain_attn_grad = attn_back(attn_norm_grad)
    input_grad = (residual_grad + input_norm_grad).astype(bf16)
    weight_grads = jnp.concatenate(
        [
            lax.dot_general(
                span_norm, qkv_grad, (((0,), (0,)), ((), ())), preferred_element_type=f32
            ),
            lax.dot_general(
                span_grad, mixed, (((0,), (0,)), ((), ())), preferred_element_type=f32
            ),
        ],
        axis=1,
    ).astype(bf16)
    weight_sum, shared_blocks, gain_blocks = reduce_wide(
        [weight_grads.reshape(groups, width // groups, -1)],
        [shared_part, gain_attn_grad.reshape(8, -1)],
        (False, False),
        sizes,
        6,
    )
    weight_blocks, shared_blocks, gain_blocks = exchange(
        [
            weight_sum.astype(bf16),
            jnp.sum(shared_blocks, axis=0),
            jnp.sum(gain_blocks, axis=0),
        ],
        (False, False, False),
        TOKEN_AXES,
        token_sizes,
        7,
    )
    weight_blocks = weight_blocks.astype(f32)

    def columns(first, count, copies):
        part = weight_blocks[:, :, first : first + count]
        part = part.reshape(slice_total // copies, copies, part.shape[1], count)
        return jnp.swapaxes(jnp.sum(part, axis=1), 0, 1).reshape(part.shape[2], -1)

    grad_w_qkv = jnp.concatenate(
        [
            columns(0, query_part, 1),
            columns(query_part, pair_part, head_copies),
            columns(query_part + pair_part, pair_part, head_copies),
        ],
        axis=1,
    )
    grad_w_out = columns(own_columns, query_part, 1)
    shared_sum = jnp.swapaxes(shared_blocks, 0, 1).reshape(shared_rows, width)
    return (
        result[None],
        input_grad[None],
        jnp.sum(gain_blocks, axis=0).reshape(width),
        grad_w_qkv,
        grad_w_out,
        shared_sum[num_experts],
        shared_sum[:num_experts].T,
        grad_expert_in,
        grad_expert_down,
    )


def solution(mesh):
    in_specs = (
        P("dp", ("blk", "ulysses"), None),
        P(),
        P(("dp", "blk"), None),
        P(("dp", "blk"), None),
        P(),
        P(),
        P(("dp", "blk"), None, None),
        P(("dp", "blk"), None, None),
        P("dp", ("blk", "ulysses"), None),
        P("dp", ("blk", "ulysses"), None),
    )
    out_specs = (
        P("dp", ("blk", "ulysses"), None),
        P("dp", ("blk", "ulysses"), None),
        P(),
        P(("dp", "blk"), None),
        P(("dp", "blk"), None),
        P(),
        P(),
        P(("dp", "blk"), None, None),
        P(("dp", "blk"), None, None),
    )
    return jax.shard_map(body, mesh=mesh, in_specs=in_specs, out_specs=out_specs, check_vma=False)
```

time: 881 us -> 428 us (0.49)
  waiting for transfers between devices: 494 us -> 20.9 us
  Pallas kernels: 0 us -> 235 us
  local copies, waits for them, and re-layouts: 98.4 us -> 30.7 us
  starting transfers between devices: 60.3 us -> 3.76 us
  blocking collectives: 49.8 us -> 0 us
  other arithmetic: 60 us -> 41.2 us
    pallas_call x0 -> x8, Pallas kernels: none -> 235 us  [the longest x2 88.3 us: gather_wide(): pl.pallas_call(functools.partial(gather_kernel, sizes, token_sizes, wide,...]
    all_to_all x12 -> x0, waiting for transfers between devices: 169 us -> none  [the longest x1 54.7 us: body(): lax.all_to_all(expert_grad, ('dp', 'blk'), split_axis=0, concat_axis=1, t...]
    psum x1 -> x0, waiting for transfers between devices: 116 us -> none  [body(): lax.psum((gain_attn_grad, gain_mix_grad, router_grad), ('dp', 'blk', 'uly...]
    all_gather x3, waiting for transfers between devices: 97.5 us -> 0.01 us  [the longest x1 0.01 us: body(): lax.all_gather(cotangent[0], EXPERT_AXES, axis=0, tiled=True)]
    reduce_scatter x2, waiting for transfers between devices: 110 us -> 15.9 us  [the longest x1 15.9 us: body(): lax.psum_scatter(weight_term(down_terms), 'ulysses', scatter_dimension=0,...]
    all_to_all x12 -> x0, starting transfers between devices: 56 us -> none  [the longest x1 5.56 us: body(): lax.all_to_all(mixed_send_grad, 'ulysses', split_axis=1, concat_axis=0, t...]
    psum x1 -> x0, blocking collectives: 39.4 us -> none  [body(): lax.psum((gain_attn_grad, gain_mix_grad, router_grad), ('dp', 'blk', 'uly...]
    gather x3 -> x0, local copies, waits for them, and re-layouts: 23 us -> none  [the longest x1 9 us: body(): expert_out.reshape(num_experts * capacity, width)[slot_index]]
  transfers between devices with their start and end apart: 20 -> 7, of which waited for: 16 -> 3; matrix products, arithmetic and copies ran while one was open for 24% -> 26% of each run, Pallas kernels for 0% -> 47%
where the time goes in v1:
time: 428 us; the launch traced here: 424 us
  Pallas kernels  235 us (55%)
  matrix products  77.6 us (18%)
  other arithmetic  41.2 us (10%)
  local copies, waits for them, and re-layouts  30.7 us (7%)
  waiting for transfers between devices  20.9 us (5%)
  between operations  15.3 us (4%)
    pallas_call x2, Pallas kernels, gather_wide(): pl.pallas_call(functools.partial(gather_kernel, sizes, token_sizes, wide,...  88.3 us
    pallas_call x2, Pallas kernels, reduce_wide(): pl.pallas_call(functools.partial(reduce_kernel, sizes, total, personal),...  87.5 us
    pallas_call x4, Pallas kernels, exchange(): pl.pallas_call(functools.partial(exchange_kernel, axes, sizes, personal),...  59.2 us
    reduce_scatter x1, waiting for transfers between devices, body(): lax.psum_scatter(weight_term(down_terms), 'ulysses', scatter_dimension=0,...  15.9 us
    unnamed x128, local copies, waits for them, and re-layouts  11.1 us
    dot_general x2, matrix products, body(): lax.dot_general(expert_grad, weight_down, (((1,), (1,)), ((), ())), prefe...  10.6 us
    dot_general x2, matrix products, body(): both_halves = jnp.dot(rows, weight_in, preferred_element_type=f32)  10.5 us
    dot_general x4, matrix products, weight_term(): lax.dot_general(left, right, (((0,), (0,)), ((), ())), preferred_element_...  9.12 us
  transfers between devices with their start and end apart: 7, of which 3 were waited for; matrix products, arithmetic and copies ran while one was open for 26% of the time, Pallas kernels for 47%

profile of v1, /device:TPU:1, one launch (start us, length us, event | category | flops | bytes accessed | tf_op | source)
XLA Modules:
  0.0 424.4 jit_solution(2262760587146393899)
XLA Ops:
  8.6 1.1 fusion.63
  9.7 1.8 fusion.58.refs_2_
  13.8 34.8 %shard_map.169 = (bf16[8,128,768]{2,1,0:T(8,128)(2,1)}, bf16[8,16,128]{2,1,0:T(8,128)(2,1)}, bf16[4,128,1024]{2,1,0:T(8,128)(2,1)}) custom-call(bf16[128,768]{1,0:T(8,128)(2,1)} %pad_maximum_fusion.16.refs_0_, bf16[16,128]{1,0:T(8,128)(2,1)} %convert_bitcast_fusion.refs_1_, bf16[128,1024]{1,0:T(8,128)(2,1)} %fusion.58.refs_2_), custom_call_target="tpu_custom_call" | custom-call | tf_op jit(solution)/shard_map/pallas_call | solution.py:317
  48.6 2.3 fusion.46
  51.4 2.1 collective-permute-start
  53.7 1.0 compare_and_fusion
  54.9 2.9 collective-permute-done
  57.8 1.6 fusion.98
  59.5 1.2 fusion.3
  60.7 2.2 copy-done.1
  62.9 1.6 fusion.36
  64.5 2.6 convolution_convert_fusion.4
  67.1 16.2 %shard_map.170 = bf16[4,128,1024]{2,1,0:T(8,128)(2,1)} custom-call(bf16[4,128,1024]{2,1,0:T(8,128)(2,1)} %bitcast.249), custom_call_target="tpu_custom_call" | custom-call | tf_op jit(solution)/shard_map/pallas_call | solution.py:227
  83.3 1.5 convert_reduce_fusion.1
  85.8 53.5 %shard_map.171 = bf16[8,128,1024]{2,1,0:T(8,128)(2,1)} custom-call(bf16[128,1024]{1,0:T(8,128)(2,1)} %multiply_convert_fusion.6.refs_0_), custom_call_target="tpu_custom_call" | custom-call | tf_op jit(solution)/shard_map/pallas_call | solution.py:317
  139.4 2.4 fusion.99
  141.9 6.1 %fusion.15 = f32[1024,1024]{0,1:T(8,128)} fusion(bf16[1024,1024]{1,0:T(8,128)(2,1)S(1)} %bitcast.243, bf16[2,1024,1024]{2,1,0:T(8,128)(2,1)} %param.16), kind=kOutput, calls=%fused_computation.30 | convolution fusion | flops 2147483648 | bytes 8388608 | tf_op jit(solution)/shard_map/dot_general | solution.py:558
  148.0 4.3 %fusion.19 = f32[1024,1024]{0,1:T(8,128)} fusion(bf16[1024,1024]{1,0:T(8,128)(2,1)S(1)} %bitcast.244, bf16[2,1024,1024]{2,1,0:T(8,128)(2,1)S(1)} %copy-done.51), kind=kOutput, calls=%fused_computation.34 | convolution fusion | flops 2147483648 | bytes 8388608 | tf_op jit(solution)/shard_map/dot_general | solution.py:558
  152.4 6.9 %multiply_convert_fusion.1 = (bf16[1024,512]{0,1:T(8,128)(2,1)}, bf16[1024,512]{0,1:T(8,128)(2,1)}, bf16[1024,512]{0,1:T(8,128)(2,1)S(1)}) fusion(f32[1024,1024]{0,1:T(8,128)} %fusion.15, bf16[2,512,1024]{2,1,0:T(8,128)(2,1)} %param.17, bf16[1,1024,1024]{2,1,0:T(8,128)(2,1)} %all-gather.9.cloned.1.call-done, f32[1024]{0:T(1024)S(1)} %bitcast.298), kind=kOutput, calls=%fused_computation.38 | convolution fusion | flops 1084751872 | bytes 10489856 | tf_op jit(solution)/shard_map/dot_general | solution.py:568
  159.3 1.3 convolution_convert_fusion.2
  161.3 1.2 copy-done.57
  162.5 3.6 multiply_convert_fusion.3
  166.2 1.3 convolution_convert_fusion.3
  167.5 1.5 pad_maximum_fusion.3
  169.1 4.1 convolution_convert_fusion
  173.2 2.4 convolution_convert_fusion.1
  175.6 2.5 pad_maximum_fusion
  179.5 1.7 copy.63
  181.5 2.7 fusion.39
  184.3 2.4 fusion.9
  186.6 15.9 %reduce-scatter.5.cloned.1.call-done = bf16[256,1024]{1,0:T(8,128)(2,1)} async-done(((bf16[1024,1024]{1,0:T(8,128)(2,1)}), bf16[256,1024]{1,0:T(8,128)(2,1)}) %reduce-scatter.5.cloned.1.call-update) | async-done | bytes 524304 | tf_op jit(solution)/shard_map/reduce_scatter | solution.py:616
  202.7 4.8 %fusion.13 = f32[1024,1024]{1,0:T(8,128)S(1)} fusion(bf16[2,1024,1024]{2,1,0:T(8,128)(2,1)} %param.16, bf16[1024,512]{0,1:T(8,128)(2,1)} %get-tuple-element.132, bf16[1024,512]{0,1:T(8,128)(2,1)} %get-tuple-element.131), kind=kOutput, calls=%fused_computation.28 | convolution fusion | flops 2151677952 | bytes 8388608 | tf_op jit(solution)/shard_map/dot_general | solution.py:581
  207.6 2.4 add_convert_fusion
  210.0 57.5 %shard_map.172 = (f32[128,1024]{1,0:T(8,128)S(1)}, f32[128,1024]{1,0:T(8,128)S(1)}, f32[8,8,128]{2,1,0:T(8,128)S(1)}) custom-call(bf16[8,128,1024]{2,1,0:T(8,128)(2,1)S(1)} %bitcast.239, bf16[8,128,1024]{2,1,0:T(8,128)(2,1)S(1)} %bitcast.240, f32[8,8,128]{2,1,0:T(8,128)S(1)} %maximum_bitcast_fusion.6.refs_2_), custom_call_target="tpu_custom_call" | custom-call | tf_op jit(solution)/shard_map/pallas_call | solution.py:407
  270.0 15.5 %shard_map.173 = (bf16[4,128,1024]{2,1,0:T(8,128)(2,1)}, f32[4,24,256]{2,1,0:T(8,128)}) custom-call(bf16[128,1024]{1,0:T(8,128)(2,1)} %fusion.95.refs_0_, f32[4,24,256]{2,1,0:T(8,128)} %bitcast.280), custom_call_target="tpu_custom_call" | custom-call | tf_op jit(solution)/shard_map/pallas_call | solution.py:227
  285.5 1.8 convolution_convert_fusion.8
  287.4 8.2 %fusion = (f32[512,2,2]{0,2,1:T(2,128)S(1)}, f32[2,1024,512,2]{2,1,3,0:T(8,128)}) fusion(f32[512,2,2,1024]{0,3,2,1:T(8,128)} %copy-done.1, f32[512,2,2]{0,2,1:T(2,128)S(1)} %log_add_fusion, bf16[512,2,2,64]{0,3,2,1:T(8,128)(2,1)S(1)} %bitcast.260, bf16[512,2,64]{0,2,1:T(8,128)(2,1)S(1)} %copy-done.29, bf16[512,2,64]{0,2,1:T(8,128)(2,1)S(1)} %bitcast.257), kind=kOutput, calls=%fused_computation.2 | convolution fusion | flops 275249152 | bytes 17317888 | tf_op jit(solution)/shard_map/while/body/eval_jaxpr/qrgd,krd->qrgk/dot_general | solution.py:112
  295.6 7.1 %fusion.2 = bf16[512,2,2,1024]{0,3,2,1:T(8,128)(2,1)S(1)} fusion(f32[2,1024,512,2]{2,1,3,0:T(8,128)} %get-tuple-element.167, f32[512,2,2,1024]{0,3,2,1:T(8,128)} %copy-done.1, f32[512,2,2]{0,2,1:T(2,128)S(1)} %get-tuple-element.166, f32[512,2,2]{0,2,1:T(2,128)S(1)} %log_add_fusion), kind=kLoop, calls=%fused_computation.4 | loop fusion | flops 8388608 | bytes 20987904 | tf_op jit(solution)/shard_map/while/body/eval_jaxpr/convert_element_type | solution.py:118
  302.7 2.1 copy-done.2
  304.8 1.4 fusion.33
  306.7 4.8 %fusion.29 = f32[1024,2,64]{0,2,1:T(8,128)S(1)} fusion(bf16[512,2,2,64]{0,3,2,1:T(8,128)(2,1)S(1)} %bitcast.261, f32[512,2,2,1024]{0,3,2,1:T(8,128)} %copy-done.1, f32[512,2,2]{0,2,1:T(2,128)S(1)} %log_add_fusion), kind=kOutput, calls=%fused_computation.62 | convolution fusion | flops 272629760 | bytes 9183232 | tf_op jit(solution)/shard_map/while/body/eval_jaxpr/qrgk,qrgd->krd/dot_general | solution.py:106
  313.9 1.4 collective-permute-start.1
  315.3 3.0 fusion.35
  319.4 1.7 copy.64
  321.6 2.0 collective-permute-done.1
  323.6 1.0 fusion.66
  325.6 3.2 convolution_convert_fusion.6
  328.8 14.1 %shard_map.174 = bf16[4,128,1024]{2,1,0:T(8,128)(2,1)} custom-call(bf16[4,128,1024]{2,1,0:T(8,128)(2,1)} %bitcast.267), custom_call_target="tpu_custom_call" | custom-call | tf_op jit(solution)/shard_map/pallas_call | solution.py:227
  343.8 1.1 copy-done.7
  345.3 30.0 %shard_map.175 = (f32[128,768]{1,0:T(8,128)S(1)}, f32[8,24,256]{2,1,0:T(8,128)S(1)}, f32[8,8,128]{2,1,0:T(8,128)S(1)}) custom-call(bf16[8,128,768]{2,1,0:T(8,128)(2,1)S(1)} %pad_maximum_fusion.4.refs_0_, f32[24,256]{1,0:T(8,128)S(1)} %reduce_sum.197.refs_1_, f32[8,128]{1,0:T(8,128)S(1)} %bitcast.241), custom_call_target="tpu_custom_call" | custom-call | tf_op jit(solution)/shard_map/pallas_call | solution.py:407
  377.2 13.4 %shard_map.176 = (bf16[4,128,768]{2,1,0:T(8,128)(2,1)}, f32[4,24,256]{2,1,0:T(8,128)}, f32[4,8,128]{2,1,0:T(8,128)}) custom-call(bf16[128,768]{1,0:T(8,128)(2,1)} %convert_element_type.219.refs_0_, f32[24,256]{1,0:T(8,128)} %reduce_sum.199.refs_1_, f32[8,128]{1,0:T(8,128)} %reduce_sum.200.refs_2_), custom_call_target="tpu_custom_call" | custom-call | tf_op jit(solution)/shard_map/pallas_call | solution.py:227
  390.6 1.3 reduce_sum.204
  391.9 1.3 convert_element_type.220
  394.0 1.8 copy.68
  395.8 1.8 copy.67
  397.6 1.1 slice_bitcast_fusion
  398.7 1.2 copy.66
  399.9 1.1 pad_maximum_fusion.9
  401.0 1.3 copy.71
  402.3 1.3 copy.69
  403.6 1.0 copy.72
  405.9 1.0 fusion.72
  406.9 4.1 convert.86
  411.0 6.6 %convert.85 = f32[2,1024,1024]{2,1,0:T(8,128)} convert(bf16[2,1024,1024]{2,1,0:T(8,128)(2,1)} %bitcast.247) | non-fusion elementwise | flops 2097152 | bytes 12582912 | tf_op jit(solution)/shard_map/reshape | solution.py:622
  (204 shorter events, 20.9 us)
Async XLA Ops:
  7.2 132.2 %copy-start = (bf16[1024,16]{0,1:T(8,128)(2,1)S(1)}, bf16[1024,16]{0,1:T(8,128)(2,1)}, u32[]{:S(2)}) copy-start(bf16[1024,16]{0,1:T(8,128)(2,1)} %param.15) | copy-start | bytes 98308
  7.2 145.2 %all-gather.9.cloned.1.call-start = ((), (), s32[]{:S(2)}) async-start(), calls=%async_computation.6 | async-start | bytes 2359296 | tf_op jit(solution)/shard_map/all_gather | solution.py:496
  9.6 41.3 %copy-start.45 = (f32[128]{0:T(128)}, f32[128]{0:T(128)S(1)}, u32[]{:S(2)}) copy-start(f32[128]{0:T(128)S(1)} %fusion.63) | copy-start | bytes 1540
  50.9 9.8 %copy-start.18 = (bf16[512,128]{0,1:T(8,128)(2,1)}, bf16[512,128]{0,1:T(8,128)(2,1)S(1)}, u32[]{:S(2)}) copy-start(bf16[512,128]{0,1:T(8,128)(2,1)S(1)} %slice.278) | copy-start | bytes 393220
  51.3 6.5 %copy-start.12 = (f32[512,32]{0,1:T(8,128)}, f32[512,32]{0,1:T(8,128)S(1)}, u32[]{:S(2)}) copy-start(f32[512,32]{0,1:T(8,128)S(1)} %get-tuple-element.158) | copy-start | bytes 196612
  51.4 8.1 %copy-start.24 = (bf16[512,2,32]{0,2,1:T(8,128)(2,1)}, bf16[512,2,32]{0,2,1:T(8,128)(2,1)S(1)}, u32[]{:S(2)}) copy-start(bf16[512,2,32]{0,2,1:T(8,128)(2,1)S(1)} %get-tuple-element.149) | copy-start | bytes 196612
  51.4 8.1 %copy-start.26 = (bf16[512,2,32]{0,2,1:T(8,128)(2,1)}, bf16[512,2,32]{0,2,1:T(8,128)(2,1)S(1)}, u32[]{:S(2)}) copy-start(bf16[512,2,32]{0,2,1:T(8,128)(2,1)S(1)} %get-tuple-element.150) | copy-start | bytes 196612
  51.4 6.4 %collective-permute-start = (bf16[2,512,2,64]{1,3,2,0:T(8,128)(2,1)S(1)}, bf16[2,512,2,64]{1,3,2,0:T(8,128)(2,1)S(1)}, u32[]{:S(2)}, u32[]{:S(2)}) collective-permute-start(bf16[2,512,2,64]{1,3,2,0:T(8,128)(2,1)S(1)} %pad_maximum_fusion.11), channel_id=1, source_target_pairs={{0,4},{1,5},{2,6},{3,7},{8,12},{9,13},{10,14},{11,15},{16,20},{17,... | collective-permute-start | bytes 786440 | tf_op jit(solution)/shard_map/ppermute | solution.py:25
  53.6 149.0 %reduce-scatter.5.cloned.1.call-start = ((), (), s32[]{:S(2)}) async-start(), calls=%async_computation.4 | async-start | bytes 2621440 | tf_op jit(solution)/shard_map/reduce_scatter | solution.py:616
  54.9 4.6 %copy-start.30 = (bf16[512,4,32]{0,2,1:T(8,128)(2,1)}, bf16[512,4,32]{0,2,1:T(8,128)(2,1)S(1)}, u32[]{:S(2)}) copy-start(bf16[512,4,32]{0,2,1:T(8,128)(2,1)S(1)} %get-tuple-element.141) | copy-start | bytes 393220
  54.9 4.6 %copy-start.32 = (bf16[512,4,32]{0,2,1:T(8,128)(2,1)}, bf16[512,4,32]{0,2,1:T(8,128)(2,1)S(1)}, u32[]{:S(2)}) copy-start(bf16[512,4,32]{0,2,1:T(8,128)(2,1)S(1)} %get-tuple-element.142) | copy-start | bytes 393220
  57.8 1.7 copy-start.34
  57.8 2.9 copy-start.28
  59.5 3.4 copy-start.1
  64.5 18.9 %copy-start.20 = (bf16[2,64,512,2]{2,1,3,0:T(8,128)(2,1)}, bf16[2,64,512,2]{2,1,3,0:T(8,128)(2,1)S(1)}, u32[]{:S(2)}) copy-start(bf16[2,64,512,2]{2,1,3,0:T(8,128)(2,1)S(1)} %fusion.36) | copy-start | bytes 786436
  67.1 17.7 %copy-start.4 = (bf16[1,128,1024]{2,1,0:T(8,128)(2,1)S(1)}, bf16[1,128,1024]{2,1,0:T(8,128)(2,1)}, u32[]{:S(2)}) copy-start(bf16[1,128,1024]{2,1,0:T(8,128)(2,1)} %param.10) | copy-start | bytes 786436
  67.1 17.9 %copy-start.42 = (f32[1024]{0:T(1024)S(1)}, f32[1024]{0:T(1024)}, u32[]{:S(2)}) copy-start(f32[1024]{0:T(1024)} %param.14) | copy-start | bytes 12292
  84.8 54.5 %copy-start.39 = (bf16[8,16,128]{2,1,0:T(8,128)(2,1)S(1)}, bf16[8,16,128]{2,1,0:T(8,128)(2,1)}, u32[]{:S(2)}) copy-start(bf16[8,16,128]{2,1,0:T(8,128)(2,1)} %get-tuple-element.88) | copy-start | bytes 98308
  85.0 56.8 %copy-start.47 = (f32[128]{0:T(128)}, f32[128]{0:T(128)S(1)}, u32[]{:S(2)}) copy-start(f32[128]{0:T(128)S(1)} %get-tuple-element.126) | copy-start | bytes 1540
  139.3 2.5 copy-start.3
  141.9 6.2 %copy-start.51 = (bf16[2,1024,1024]{2,1,0:T(8,128)(2,1)S(1)}, bf16[2,1024,1024]{2,1,0:T(8,128)(2,1)}, u32[]{:S(2)}) copy-start(bf16[2,1024,1024]{2,1,0:T(8,128)(2,1)} %param.16) | copy-start | bytes 12582916
  152.4 7.0 %copy-start.53 = (bf16[1,1024,1024]{2,1,0:T(8,128)(2,1)S(1)}, bf16[1,1024,1024]{2,1,0:T(8,128)(2,1)}, u32[]{:S(2)}) copy-start(bf16[1,1024,1024]{2,1,0:T(8,128)(2,1)} %all-gather.9.cloned.1.call-done) | copy-start | bytes 6291460
  159.3 2.0 copy-start.36
  159.3 3.2 copy-start.57
  169.1 126.5 %reduce-scatter.3.cloned.1.call-start = ((), (), s32[]{:S(2)}) async-start(), calls=%async_computation.2 | async-start | bytes 5242880 | tf_op jit(solution)/shard_map/reduce_scatter | solution.py:613
  169.1 4.1 copy-start.58
  169.1 4.1 copy-start.60
  178.1 3.1 copy-start.8
  178.1 3.3 copy-start.17
  178.1 228.8 %all-gather.7.cloned.1.call-start = ((), (), s32[]{:S(2)}) async-start(), calls=%async_computation.5 | async-start | bytes 2621440 | tf_op jit(solution)/shard_map/all_gather | solution.py:625
  181.5 2.7 copy-start.37
  181.5 2.7 copy-start.54
  181.5 2.8 copy-start.56
  202.6 4.9 %copy-start.49 = (f32[8]{0:T(128)S(1)}, f32[8]{0:T(128)}, u32[]{:S(2)}) copy-start(f32[8]{0:T(128)} %pad.27.clone) | copy-start | bytes 100
  202.6 4.9 %copy-start.50 = (f32[8]{0:T(128)S(1)}, f32[8]{0:T(128)}, u32[]{:S(2)}) copy-start(f32[8]{0:T(128)} %pad.26.clone) | copy-start | bytes 100
  202.6 208.4 %all-gather.5.cloned.1.call-start = ((), (), s32[]{:S(2)}) async-start(), calls=%async_computation.3 | async-start | bytes 5242880 | tf_op jit(solution)/shard_map/all_gather | solution.py:620
  202.7 4.9 %copy-start.52 = (bf16[2,1024,1024]{2,1,0:T(8,128)(2,1)S(1)}, bf16[2,1024,1024]{2,1,0:T(8,128)(2,1)}, u32[]{:S(2)}) copy-start(bf16[2,1024,1024]{2,1,0:T(8,128)(2,1)} %param.16) | copy-start | bytes 12582916
  202.7 4.9 %copy-start.59 = (bf16[1024,512]{0,1:T(8,128)(2,1)S(1)}, bf16[1024,512]{0,1:T(8,128)(2,1)}, u32[]{:S(2)}) copy-start(bf16[1024,512]{0,1:T(8,128)(2,1)} %get-tuple-element.129) | copy-start | bytes 3145732
  202.7 4.9 %copy-start.61 = (bf16[1024,512]{0,1:T(8,128)(2,1)S(1)}, bf16[1024,512]{0,1:T(8,128)(2,1)}, u32[]{:S(2)}) copy-start(bf16[1024,512]{0,1:T(8,128)(2,1)} %get-tuple-element.130) | copy-start | bytes 3145732
  210.0 57.6 %copy-start.9 = (bf16[128,1024]{1,0:T(8,128)(2,1)S(1)}, bf16[128,1024]{1,0:T(8,128)(2,1)}, u32[]{:S(2)}) copy-start(bf16[128,1024]{1,0:T(8,128)(2,1)} %multiply_convert_fusion.6.refs_0_) | copy-start | bytes 786436
  267.5 1.6 copy-start.48
  267.5 1.6 copy-start.10
  268.4 19.0 %copy-start.5 = (f32[128,1024]{1,0:T(8,128)}, f32[128,1024]{1,0:T(8,128)S(1)}, u32[]{:S(2)}) copy-start(f32[128,1024]{1,0:T(8,128)S(1)} %get-tuple-element.165) | copy-start | bytes 1572868
  268.4 19.0 %copy-start.19 = (bf16[512,128]{0,1:T(8,128)(2,1)S(1)}, bf16[512,128]{0,1:T(8,128)(2,1)}, u32[]{:S(2)}) copy-start(bf16[512,128]{0,1:T(8,128)(2,1)} %copy-done.18) | copy-start | bytes 393220
  268.4 19.0 %copy-start.29 = (bf16[512,2,64]{0,2,1:T(8,128)(2,1)S(1)}, bf16[512,2,64]{0,2,1:T(8,128)(2,1)}, u32[]{:S(2)}) copy-start(bf16[512,2,64]{0,2,1:T(8,128)(2,1)} %copy-done.28) | copy-start | bytes 393220
  295.6 9.2 %copy-start.31 = (bf16[512,4,32]{0,2,1:T(8,128)(2,1)S(1)}, bf16[512,4,32]{0,2,1:T(8,128)(2,1)}, u32[]{:S(2)}) copy-start(bf16[512,4,32]{0,2,1:T(8,128)(2,1)} %copy-done.30) | copy-start | bytes 393220
  295.6 9.2 %copy-start.33 = (bf16[512,4,32]{0,2,1:T(8,128)(2,1)S(1)}, bf16[512,4,32]{0,2,1:T(8,128)(2,1)}, u32[]{:S(2)}) copy-start(bf16[512,4,32]{0,2,1:T(8,128)(2,1)} %copy-done.32) | copy-start | bytes 393220
  302.7 2.1 copy-start.2
  311.9 3.4 copy-start.25
  312.0 3.4 copy-start.27
  312.0 3.4 copy-start.35
  313.9 4.5 %copy-start.13 = (f32[512,32]{0,1:T(8,128)S(1)}, f32[512,32]{0,1:T(8,128)}, u32[]{:S(2)}) copy-start(f32[512,32]{0,1:T(8,128)} %copy-done.12) | copy-start | bytes 196612
  313.9 9.7 %collective-permute-start.1 = (bf16[2,512,2,64]{1,3,2,0:T(8,128)(2,1)}, bf16[2,512,2,64]{1,3,2,0:T(8,128)(2,1)}, u32[]{:S(2)}, u32[]{:S(2)}) collective-permute-start(bf16[2,512,2,64]{1,3,2,0:T(8,128)(2,1)} %fusion.71), channel_id=1, source_target_pairs={{4,0},{5,1},{6,2},{7,3},{12,8},{13,9},{14,10},{15,11},{20,16},{21,... | collective-permute-start | bytes 786440 | tf_op jit(solution)/shard_map/ppermute | solution.py:25
  318.4 2.7 copy-start.41
  318.4 2.7 copy-start.21
  321.1 2.5 copy-start.15
  325.6 17.3 %copy-start.23 = (bf16[1024,512]{1,0:T(8,128)(2,1)S(1)}, bf16[1024,512]{1,0:T(8,128)(2,1)}, u32[]{:S(2)}) copy-start(bf16[1024,512]{1,0:T(8,128)(2,1)} %copy.63) | copy-start | bytes 3145732
  325.6 17.3 %copy-start.38 = (bf16[512,256]{1,0:T(8,128)(2,1)S(1)}, bf16[512,256]{1,0:T(8,128)(2,1)}, u32[]{:S(2)}) copy-start(bf16[512,256]{1,0:T(8,128)(2,1)} %copy.60) | copy-start | bytes 786436
  325.6 17.3 %copy-start.40 = (bf16[512,128]{1,0:T(8,128)(2,1)S(1)}, bf16[512,128]{1,0:T(8,128)(2,1)}, u32[]{:S(2)}) copy-start(bf16[512,128]{1,0:T(8,128)(2,1)} %copy.62) | copy-start | bytes 393220
  343.7 1.4 copy-start.44
  401.0 4.9 %copy-start.46 = (f32[128]{0:T(128)S(1)}, f32[128]{0:T(128)}, u32[]{:S(2)}) copy-start(f32[128]{0:T(128)} %copy-done.45) | copy-start | bytes 1540
  401.0 4.9 %copy-start.6 = (f32[128,1024]{1,0:T(8,128)S(1)}, f32[128,1024]{1,0:T(8,128)}, u32[]{:S(2)}) copy-start(f32[128,1024]{1,0:T(8,128)} %copy-done.5) | copy-start | bytes 1572868
  402.3 2.3 copy-start.43
  402.3 3.6 copy-start.11
  (5 other events, 6.3 us)
Sparse Core Ops, SparseCore 0:
  53.7 69.4 all-gather.8
  169.2 33.3 reduce-scatter.4
  205.8 44.5 reduce-scatter.2
  251.8 22.9 all-gather.6
  295.7 34.3 all-gather.4
